TPU v7x, 512 devices: a whole 4x8x8 slice. The times are simulated.
512 devices in a mesh: chan: 64 (over x, y, core), tm: 8 (over z).
Axes of the slice: x: 4, y: 8, z: 8, core: 2. Of those that a mesh axis runs over, the one named last changes fastest.
Arguments:
- spectra: bfloat16 [16384, 2048], P('chan', 'tm'), may hold values from -6 to 6
- coarse_delay: int32 [16384, 64], P('chan'), may hold values from 0 to 95, as said below
- fine_delay: int32 [64, 64, 32], P(None, 'chan'), may hold values from 0 to 31, as said below
- widths: int32 [8], replicated, may hold values from 1 to 128, as said below
Outputs:
- boxcars: bfloat16 [8, 2048, 2048], P(None, 'chan', 'tm')
Inputs may be any that keep to these rules, and one draw needn't show every extreme that they name: `coarse_delay`: every entry is an integer delay; the value 95 occurs. `fine_delay`: every entry is an integer delay; the value 31 occurs. `widths`: the width 128 occurs.
All inputs are finite; a program needn't handle non-finite values.
Results may differ from a plain program's by a relative error of at most 0.0051.
Values may be sent and summed in bfloat16 or wider, within the bound.
No kernel may reach another device: no remote copies, remote signals or barrier semaphores. Data moves between devices by JAX's collectives and lax.ppermute only.
A program may use at most 64 MiB of HBM per device.

v0:
```python
import math

import jax
import jax.numpy as jnp
from jax import lax
from jax.sharding import PartitionSpec as P

CHANNELS = 16384
D1MAX = 95
D2MAX = 31
WMAX = 128


def passed_along(value, axis, steps):
    count = lax.axis_size(axis)
    first, last = (max(0, -steps), min(count, count - steps))
    return lax.ppermute(value, axis, [(source, source + steps) for source in range(first, last)])


def first_section(extended, coarse_delay, span):
    nblk = coarse_delay.shape[1]
    group = 8
    by_block = coarse_delay.T

    def turn(index, total):
        base = index * group
        lifted = jnp.stack(
            [lax.dynamic_slice_in_dim(extended, base + step, span, 1) for step in range(group)],
            axis=0,
        )
        levels = base + jnp.arange(group, dtype=jnp.int32)
        selector = (by_block[:, None, :] == levels[None, :, None]).astype(jnp.bfloat16)
        return total + jnp.einsum(
            "bic,ict->bt", selector, lifted, preferred_element_type=jnp.float32
        )

    total = lax.fori_loop(0, (D1MAX + 1) // group, turn, jnp.zeros((nblk, span), jnp.float32))
    return total.astype(jnp.bfloat16)


def second_section(received, fine_delay, length):
    levels = jnp.arange(D2MAX + 1, dtype=jnp.int32)

    def one_block(item):
        sub, fine = item
        lifted = jnp.stack([sub[:, step : step + length] for step in range(D2MAX + 1)], axis=1)
        selector = (fine.T[:, :, None] == levels[None, None, :]).astype(jnp.bfloat16)
        return jnp.einsum("jsk,skt->jt", selector, lifted, preferred_element_type=jnp.float32)

    series = lax.map(one_block, (jnp.swapaxes(received, 0, 1), jnp.swapaxes(fine_delay, 0, 1)))
    return series.reshape(-1, length)


def per_device(spectra, coarse_delay, fine_delay, widths):
    steps = spectra.shape[1]
    margin = D1MAX + D2MAX
    following = passed_along(spectra[:, :margin], "tm", -1)
    extended = jnp.concatenate([spectra, following], axis=1)
    span = steps + D2MAX
    subbands = first_section(extended, coarse_delay, span)
    groups = lax.axis_size("chan")
    blocks = coarse_delay.shape[1] // groups
    received = lax.all_to_all(
        subbands.reshape(groups, blocks, span), "chan", split_axis=0, concat_axis=0, tiled=True
    )
    series = second_section(received, fine_delay, steps) * (1.0 / math.sqrt(CHANNELS))
    tail = passed_along(series[:, : WMAX - 1], "tm", -1)
    longer = jnp.concatenate([series, tail], axis=1)
    prefix = jnp.concatenate(
        [jnp.zeros((longer.shape[0], 1), jnp.float32), jnp.cumsum(longer, axis=1)], axis=1
    )

    def one_width(width):
        upper = lax.dynamic_slice_in_dim(prefix, width, steps, 1)
        return ((upper - prefix[:, :steps]) / jnp.sqrt(width.astype(jnp.float32))).astype(
            jnp.bfloat16
        )

    return lax.map(one_width, widths)


def solution(mesh):
    return jax.shard_map(
        per_device,
        mesh=mesh,
        in_specs=(P("chan", "tm"), P("chan", None), P(None, "chan", None), P()),
        out_specs=P(None, "chan", "tm"),
        check_vma=False,
    )
```

profile of v0, /device:TPU:192, one launch (start us, length us, event | category | flops | bytes accessed | tf_op | source)
XLA Modules:
  0.0 90.5 jit_solution(9288998454221435629)
XLA Ops:
  0.0 1.0 %copy.17 = bf16[256,256]{0,1:T(8,128)(2,1)S(1)} copy(bf16[256,256]{1,0:T(8,128)(2,1)} %param.8) | data formatting | bytes 262144 | tf_op args[0]
  1.0 1.9 %collective-permute-start = (bf16[256,126]{0,1:T(8,128)(2,1)S(1)}, bf16[256,126]{0,1:T(8,128)(2,1)S(1)}, u32[]{:S(2)}, u32[]{:S(2)}) collective-permute-start(bf16[256,126]{0,1:T(8,128)(2,1)S(1)} %slice.183), channel_id=1, source_target_pairs={{1,0},{2,1},{3,2},{4,3},{5,4},{6,5},{7,6},{9,8},{10,9},{11,10},{12... | collective-permute-start | bytes 193544 | tf_op jit(solution)/shard_map/ppermute | solution.py:17
  3.0 5.8 %collective-permute-done = bf16[256,126]{0,1:T(8,128)(2,1)S(1)} collective-permute-done((bf16[256,126]{0,1:T(8,128)(2,1)S(1)}, bf16[256,126]{0,1:T(8,128)(2,1)S(1)}, u32[]{:S(2)}, u32[]{:S(2)}) %collective-permute-start) | collective-permute-done | bytes 64544 | tf_op jit(solution)/shard_map/ppermute | solution.py:17
  8.8 16.8 %while.31 = (s32[]{:T(128)}, f32[64,287]{1,0:T(8,128)S(1)}, s32[64,256]{1,0:T(8,128)}, bf16[256,382]{0,1:T(8,128)(2,1)S(1)}, s32[]{:T(128)}, /*index=5*/s32[]{:T...) while((s32[]{:T(128)}, f32[64,287]{1,0:T(8,128)S(1)}, ...), condition=%wide.region_1.0_spmd.clone, body=%wide.region_0.0_spmd.clone.sunk | while | flops 75403176 | bytes 4009655 | solution.py:37
  9.3 0.3 copy-done
  9.6 0.5 fusion.15
  10.7 0.3 copy-done
  11.0 0.5 fusion.15
  12.1 0.3 copy-done
  12.4 0.5 fusion.15
  13.5 0.3 copy-done
  13.8 0.5 fusion.15
  14.9 0.3 copy-done
  15.2 0.5 fusion.15
  16.3 0.3 copy-done
  16.6 0.5 fusion.15
  17.7 0.3 copy-done
  18.0 0.5 fusion.15
  19.1 0.3 copy-done
  19.4 0.5 fusion.15
  20.8 0.5 fusion.15
  21.9 0.3 copy-done
  22.2 0.5 fusion.15
  23.3 0.3 copy-done
  23.6 0.5 fusion.15
  24.7 0.3 copy-done
  25.0 0.5 fusion.15
  25.7 20.5 %all_to_all.5 = bf16[64,1,287]{2,1,0:T(2,128)(2,1)S(1)} all-to-all(bf16[64,1,287]{2,1,0:T(2,128)(2,1)S(1)} %copy.18), channel_id=1, replica_groups=mesh['chan'=64,'tm'=8] {'chan'}, dimensions={0} | all-to-all | bytes 73472 | tf_op jit(solution)/shard_map/all_to_all | solution.py:63
  49.1 1.9 %collective-permute-start.1 = (f32[32,127]{1,0:T(8,128)S(1)}, f32[32,127]{1,0:T(8,128)S(1)}, u32[]{:S(2)}, u32[]{:S(2)}) collective-permute-start(f32[32,127]{1,0:T(8,128)S(1)} %slice.216), channel_id=1, source_target_pairs={{1,0},{2,1},{3,2},{4,3},{5,4},{6,5},{7,6},{9,8},{10,9},{11,10},{12... | collective-permute-start | bytes 48776 | tf_op jit(solution)/shard_map/ppermute | solution.py:17
  51.0 4.9 %collective-permute-done.1 = f32[32,127]{1,0:T(8,128)S(1)} collective-permute-done((f32[32,127]{1,0:T(8,128)S(1)}, f32[32,127]{1,0:T(8,128)S(1)}, u32[]{:S(2)}, u32[]{:S(2)}) %collective-permute-start.1) | collective-permute-done | bytes 16288 | tf_op jit(solution)/shard_map/ppermute | solution.py:17
  55.9 0.9 reduce-window.6
  57.2 33.3 %while.30 = (s32[]{:T(128)}, bf16[8,32,256]{2,1,0:T(8,128)(2,1)}, s32[8]{0:T(128)S(1)}, f32[32,384]{1,0:T(8,128)S(1)}, s32[]{:T(128)}, /*index=5*/s32[]{:T(128)}, s32[]{:T(128)}) while((s32[]{:T(128)}, bf16[8,32,256]{2,1,0:T(8,128)(2,1)}, s32[8]{0:T(128)S(1)}, f32[32,384]{1,0:T(8,128)S(1)}, s32[]{:T(128)}, /*index=5*/s32[]{:T(128)}, ...), condition=%wide.region_5.6_spmd, body=%wide.region_4.5_spmd.sunk | while | flops 24582 | bytes 82579 | solution.py:79
  57.2 0.7 dynamic_slice.123
  60.7 0.7 bitcast_dynamic-update-slice_fusion.18
  61.4 0.7 dynamic_slice.123
  64.8 0.7 bitcast_dynamic-update-slice_fusion.18
  65.5 0.7 dynamic_slice.123
  69.0 0.7 bitcast_dynamic-update-slice_fusion.18
  69.7 0.7 dynamic_slice.123
  73.2 0.7 bitcast_dynamic-update-slice_fusion.18
  73.8 0.7 dynamic_slice.123
  77.3 0.7 bitcast_dynamic-update-slice_fusion.18
  78.0 0.7 dynamic_slice.123
  81.5 0.7 bitcast_dynamic-update-slice_fusion.18
  82.2 0.7 dynamic_slice.123
  85.6 0.7 bitcast_dynamic-update-slice_fusion.18
  86.3 0.7 dynamic_slice.123
  89.8 0.7 bitcast_dynamic-update-slice_fusion.18
  (171 shorter events, 8.0 us)
Async XLA Ops:
  1.0 7.7 %collective-permute-start = (bf16[256,126]{0,1:T(8,128)(2,1)S(1)}, bf16[256,126]{0,1:T(8,128)(2,1)S(1)}, u32[]{:S(2)}, u32[]{:S(2)}) collective-permute-start(bf16[256,126]{0,1:T(8,128)(2,1)S(1)} %slice.183), channel_id=1, source_target_pairs={{1,0},{2,1},{3,2},{4,3},{5,4},{6,5},{7,6},{9,8},{10,9},{11,10},{12... | collective-permute-start | bytes 193544 | tf_op jit(solution)/shard_map/ppermute | solution.py:17
  8.8 0.8 copy-start
  10.2 0.8 copy-start
  11.6 0.8 copy-start
  13.0 0.8 copy-start
  14.4 0.8 copy-start
  15.8 0.8 copy-start
  17.2 0.8 copy-start
  18.6 0.8 copy-start
  20.0 0.8 copy-start
  21.4 0.8 copy-start
  22.8 0.8 copy-start
  24.2 0.8 copy-start
  25.7 23.1 %copy-start.1 = (s32[64,1,32]{0,2,1:T(8,128)S(1)}, s32[64,1,32]{0,2,1:T(8,128)}, u32[]{:S(2)}) copy-start(s32[64,1,32]{0,2,1:T(8,128)} %param.10) | copy-start | bytes 24580
  47.8 9.4 %copy-start.2 = (s32[8]{0:T(128)S(1)}, s32[8]{0:T(128)}, u32[]{:S(2)}) copy-start(s32[8]{0:T(128)} %param.11) | copy-start | bytes 100
  49.1 6.8 %collective-permute-start.1 = (f32[32,127]{1,0:T(8,128)S(1)}, f32[32,127]{1,0:T(8,128)S(1)}, u32[]{:S(2)}, u32[]{:S(2)}) collective-permute-start(f32[32,127]{1,0:T(8,128)S(1)} %slice.216), channel_id=1, source_target_pairs={{1,0},{2,1},{3,2},{4,3},{5,4},{6,5},{7,6},{9,8},{10,9},{11,10},{12... | collective-permute-start | bytes 48776 | tf_op jit(solution)/shard_map/ppermute | solution.py:17
where the time goes:
time: 91.6 us; the launch traced here: 90.5 us
  loops' own time  24.4 us (27%)
  blocking collectives  20.5 us (22%)
  local copies, waits for them, and re-layouts  17.6 us (19%)
  waiting for transfers between devices  10.7 us (12%)
  matrix products  6.63 us (7%)
  other arithmetic  6.62 us (7%)
  starting transfers between devices  3.84 us (4%)
    another operation x1, loops' own time, per_device(): return lax.map(one_width, widths)  22.5 us
    all_to_all x1, blocking collectives, per_device(): lax.all_to_all(subbands.reshape(groups, blocks, span), 'chan', split_axis...  20.5 us
    ppermute x2, waiting for transfers between devices, passed_along(): lax.ppermute(value, axis, [(source, source + steps) for source in range(f...  10.7 us
    while x108, local copies, waits for them, and re-layouts  7.89 us
    dot_general x12, matrix products, turn(): jnp.einsum('bic,ict->bt', selector, lifted, preferred_element_type=jnp.fl...  6.33 us
    dynamic_update_slice x8, other arithmetic, per_device(): return lax.map(one_width, widths)  5.55 us
    dynamic_slice x8, local copies, waits for them, and re-layouts, per_device(): return lax.map(one_width, widths)  5.31 us
    ppermute x2, starting transfers between devices, passed_along(): lax.ppermute(value, axis, [(source, source + steps) for source in range(f...  3.84 us
  transfers between devices with their start and end apart: 2, of which 2 were waited for; matrix products, arithmetic and copies ran while one was open for 0% of the time, Pallas kernels for 0%

commit v1 on v0

v1 whole, which is shorter than its diff:
```python
import functools
import math

import jax
import jax.numpy as jnp
from jax import lax
from jax.experimental import pallas as pl
from jax.experimental.pallas import tpu as pltpu
from jax.sharding import PartitionSpec as P

CHANNELS = 16384
D1MAX = 95
D2MAX = 31
WMAX = 128
LANES = 128
R1 = 8
Q1 = (D1MAX + 1) // R1
R2 = 4
Q2 = (D2MAX + 1) // R2
CHUNKS = 4


def shift_left(x, by):
    if by == 0:
        return x
    return jnp.concatenate([x[:, by:], jnp.zeros((x.shape[0], by), x.dtype)], axis=1)


def shift_right(x, by):
    if by == 0:
        return x
    return jnp.concatenate([jnp.zeros((x.shape[0], by), x.dtype), x[:, :-by]], axis=1)


def one_hot(delay, level):
    return jnp.where(delay == level, jnp.ones((), jnp.bfloat16), jnp.zeros((), jnp.bfloat16))


def level_sums(delay, spectra, shift, acc_ref):
    for r in range(R1):
        selector = jnp.concatenate([one_hot(delay, float(R1 * q + r)) for q in range(Q1)], axis=0)
        part = jnp.dot(selector, shift(spectra, r), preferred_element_type=jnp.float32)
        if r == 0:
            acc_ref[...] = part
        else:
            acc_ref[...] += part


def own_kernel(spectra_ref, delay_ref, out_ref, acc_ref):
    nblk, steps = out_ref.shape
    delay = delay_ref[...].astype(jnp.bfloat16)
    level_sums(delay, spectra_ref[...], shift_left, acc_ref)
    total = acc_ref[0:nblk, :]
    for q in range(1, Q1):
        total = total + shift_left(acc_ref[nblk * q : nblk * (q + 1), :], R1 * q)
    out_ref[...] = total


def next_kernel(own_ref, spectra_ref, delay_ref, out_ref, acc_ref, rows_ref):
    nblk, steps = own_ref.shape
    delay = delay_ref[...].astype(jnp.bfloat16)
    level_sums(delay, spectra_ref[...], lambda x, r: shift_right(x, R1 - r), acc_ref)
    total = jnp.zeros((nblk, steps + LANES), jnp.float32)
    for q in range(Q1):
        left = LANES - R1 * (q + 1)
        pieces = [acc_ref[nblk * q : nblk * (q + 1), :], jnp.zeros((nblk, LANES - left), jnp.float32)]
        if left:
            pieces = [jnp.zeros((nblk, left), jnp.float32)] + pieces
        total = total + jnp.concatenate(pieces, axis=1)
    rows_ref[pl.ds(0, nblk, stride=CHUNKS), :] = own_ref[:, :LANES]
    rows_ref[pl.ds(1, nblk, stride=CHUNKS), :] = own_ref[:, LANES:] + total[:, :LANES]
    rows_ref[pl.ds(2, nblk, stride=CHUNKS), :] = total[:, LANES : 2 * LANES]
    rows_ref[pl.ds(3, nblk, stride=CHUNKS), :] = total[:, 2 * LANES :]
    out_ref[...] = rows_ref[...].astype(jnp.bfloat16)


def trial_kernel(widths_ref, sub_ref, delay_ref, out_ref, rows_ref):
    trials, nsub = delay_ref.shape
    rows_ref[...] = sub_ref[...].astype(jnp.float32)
    sub = jnp.concatenate(
        [rows_ref[pl.ds(m, nsub, stride=CHUNKS), :] for m in range(CHUNKS)], axis=1
    ).astype(jnp.bfloat16)
    shifted = jnp.concatenate([shift_left(sub, r) for r in range(R2)], axis=0)
    delay = delay_ref[...]
    delay = jnp.concatenate([delay - r for r in range(R2)], axis=1).astype(jnp.bfloat16)
    selector = jnp.concatenate([one_hot(delay, float(R2 * q)) for q in range(Q2)], axis=0)
    parts = jnp.dot(selector, shifted, preferred_element_type=jnp.float32)
    series = parts[:trials]
    for q in range(1, Q2):
        series = series + shift_left(parts[trials * q : trials * (q + 1)], R2 * q)
    length = 3 * LANES
    series = series[:, :length] * (1.0 / math.sqrt(CHANNELS))
    high = series.astype(jnp.bfloat16)
    rest = series - high.astype(jnp.float32)
    middle = rest.astype(jnp.bfloat16)
    low = (rest - middle.astype(jnp.float32)).astype(jnp.bfloat16)
    before = lax.broadcasted_iota(jnp.int32, (length, length), 0)
    after = lax.broadcasted_iota(jnp.int32, (length, length), 1)
    triangle = jnp.where(before < after, 1.0, 0.0).astype(jnp.bfloat16)
    sums = jnp.dot(
        jnp.concatenate([high, middle, low], axis=0), triangle, preferred_element_type=jnp.float32
    )
    prefix = sums[:trials] + (sums[trials : 2 * trials] + sums[2 * trials :])
    columns = [prefix[:, LANES * m : LANES * (m + 1)] for m in range(3)]
    lane = lax.broadcasted_iota(jnp.int32, (trials, LANES), 1)
    for index in range(out_ref.shape[0]):
        width = widths_ref[index]
        turned = [pltpu.roll(column, LANES - width, 1) for column in columns]
        scale = 1.0 / jnp.sqrt(jnp.full((trials, LANES), width.astype(jnp.float32)))
        inside = lane < LANES - width
        for m in range(2):
            upper = jnp.where(inside, turned[m], turned[m + 1])
            out_ref[index, :, LANES * m : LANES * (m + 1)] = (
                (upper - columns[m]) * scale
            ).astype(jnp.bfloat16)


VMEM = pl.BlockSpec(memory_space=pltpu.VMEM)
SMEM = pl.BlockSpec(memory_space=pltpu.SMEM)
PARAMS = pltpu.CompilerParams(vmem_limit_bytes=16 * 1024 * 1024)


def per_device(spectra, coarse_delay, fine_delay, widths):
    channels, steps = spectra.shape
    nblk = coarse_delay.shape[1]
    nsub, _, trials = fine_delay.shape
    count = lax.axis_size("tm")
    following = lax.ppermute(spectra, "tm", [(z + 1, z) for z in range(count - 1)])
    by_block = coarse_delay.T
    sums = pltpu.VMEM((Q1 * nblk, steps), jnp.float32)
    flops = 2 * (D1MAX + 1) * nblk * channels * steps
    own = pl.pallas_call(
        own_kernel,
        out_shape=jax.ShapeDtypeStruct((nblk, steps), jnp.float32),
        in_specs=[VMEM] * 2,
        out_specs=VMEM,
        scratch_shapes=[sums],
        compiler_params=PARAMS,
        cost_estimate=pl.CostEstimate(flops=flops, bytes_accessed=1 << 20, transcendentals=0),
        name="own_sums",
    )(spectra, by_block)
    subbands = pl.pallas_call(
        next_kernel,
        out_shape=jax.ShapeDtypeStruct((nblk * CHUNKS, LANES), jnp.bfloat16),
        in_specs=[VMEM] * 3,
        out_specs=VMEM,
        scratch_shapes=[sums, pltpu.VMEM((nblk * CHUNKS, LANES), jnp.float32)],
        compiler_params=PARAMS,
        cost_estimate=pl.CostEstimate(flops=flops, bytes_accessed=1 << 20, transcendentals=0),
        name="next_sums",
    )(own, following, by_block)
    received = lax.all_to_all(subbands, "chan", split_axis=0, concat_axis=0, tiled=True)
    return pl.pallas_call(
        trial_kernel,
        out_shape=jax.ShapeDtypeStruct((widths.shape[0], trials, steps), jnp.bfloat16),
        in_specs=[SMEM, VMEM, VMEM],
        out_specs=VMEM,
        scratch_shapes=[pltpu.VMEM((nsub * CHUNKS, LANES), jnp.float32)],
        compiler_params=PARAMS,
        name="trials",
    )(widths, received, fine_delay.reshape(nsub, trials).T)


def solution(mesh):
    return jax.shard_map(
        per_device,
        mesh=mesh,
        in_specs=(P("chan", "tm"), P("chan", None), P(None, "chan", None), P()),
        out_specs=P(None, "chan", "tm"),
        check_vma=False,
    )
```

time: 91.6 us -> 33.6 us (0.37)
  the two profiles are of different devices: /device:TPU:192 before, /device:TPU:1 now
where the time goes in v1:
time: 33.6 us; the launch traced here: 33 us
  blocking collectives  21.8 us (65%)
  Pallas kernels  4.24 us (13%)
  waiting for transfers between devices  3.24 us (10%)
  local copies, waits for them, and re-layouts  2.4 us (7%)
  starting transfers between devices  1.28 us (4%)
    all_to_all x1, blocking collectives, per_device(): lax.all_to_all(subbands, 'chan', split_axis=0, concat_axis=0, tiled=True)  21.8 us
    ppermute x1, waiting for transfers between devices, per_device(): lax.ppermute(spectra, 'tm', [(z + 1, z) for z in range(count - 1)])  3.24 us
    unnamed x8, local copies, waits for them, and re-layouts  2.4 us
    pallas_call x1, Pallas kernels, per_device(): pl.pallas_call(trial_kernel, out_shape=jax.ShapeDtypeStruct((widths.shape...  1.97 us
    ppermute x1, starting transfers between devices, per_device(): lax.ppermute(spectra, 'tm', [(z + 1, z) for z in range(count - 1)])  1.28 us
    pallas_call x1, Pallas kernels, per_device(): pl.pallas_call(next_kernel, out_shape=jax.ShapeDtypeStruct((nblk * CHUNKS...  1.17 us
    pallas_call x1, Pallas kernels, per_device(): pl.pallas_call(own_kernel, out_shape=jax.ShapeDtypeStruct((nblk, steps),...  1.1 us
  transfers between devices with their start and end apart: 1, of which 1 were waited for; matrix products, arithmetic and copies ran while one was open for 0% of the time, Pallas kernels for 3%

profile of v1, /device:TPU:1, one launch (start us, length us, event | category | flops | bytes accessed | tf_op | source)
XLA Modules:
  0.0 33.0 jit_solution(9787203119445660913)
XLA Ops:
  0.0 1.3 %collective-permute-start = (bf16[256,256]{1,0:T(8,128)(2,1)}, bf16[256,256]{1,0:T(8,128)(2,1)S(1)}, u32[]{:S(2)}, u32[]{:S(2)}) collective-permute-start(bf16[256,256]{1,0:T(8,128)(2,1)} %spectra_ref.1), channel_id=1, source_target_pairs={{1,0},{2,1},{3,2},{4,3},{5,4},{6,5},{7,6},{9,8},{10,9},{11,10},{12... | collective-permute-start | bytes 393224 | tf_op jit(solution)/shard_map/ppermute | solution.py:128
  1.3 0.0 copy-start.2
  1.3 0.9 %copy-done.2 = bf16[256,256]{1,0:T(8,128)(2,1)S(1)} copy-done((bf16[256,256]{1,0:T(8,128)(2,1)S(1)}, bf16[256,256]{1,0:T(8,128)(2,1)}, u32[]{:S(2)}) %copy-start.2) | copy-done | bytes 131096
  2.2 0.0 copy-start.3
  2.2 0.8 %copy-done.3 = s32[256,64]{0,1:T(8,128)S(1)} copy-done((s32[256,64]{0,1:T(8,128)S(1)}, s32[256,64]{0,1:T(8,128)}, u32[]{:S(2)}) %copy-start.3) | copy-done | bytes 65560
  3.0 1.1 %own_sums.1.own_ref = f32[64,256]{1,0:T(8,128)S(1)} custom-call(bf16[256,256]{1,0:T(8,128)(2,1)S(1)} %copy-done.2, s32[64,256]{1,0:T(8,128)S(1)} %bitcast.9), custom_call_target="tpu_custom_call" | custom-call | flops 805306368 | bytes 1048576 | tf_op jit(solution)/shard_map/own_sums/pallas_call | solution.py:132
  4.1 3.2 %collective-permute-done.spectra_ref = bf16[256,256]{1,0:T(8,128)(2,1)S(1)} collective-permute-done((bf16[256,256]{1,0:T(8,128)(2,1)}, bf16[256,256]{1,0:T(8,128)(2,1)S(1)}, u32[]{:S(2)}, u32[]{:S(2)}) %collective-permute-start) | collective-permute-done | bytes 131104 | tf_op jit(solution)/shard_map/ppermute | solution.py:128
  7.4 1.2 %next_sums.1 = bf16[256,128]{1,0:T(8,128)(2,1)S(1)} custom-call(f32[64,256]{1,0:T(8,128)S(1)} %own_sums.1.own_ref, bf16[256,256]{1,0:T(8,128)(2,1)S(1)} %collective-permute-done.spectra_ref, s32[64,256]{1,0:T(8,128)S(1)} %bitcast.10), custom_call_target="tpu_custom_call" | custom-call | flops 805306368 | bytes 1048576 | tf_op jit(solution)/shard_map/next_sums/pallas_call | solution.py:142
  8.6 0.0 copy-start
  8.6 21.8 %all_to_all.11 = bf16[64,4,128]{2,1,0:T(4,128)(2,1)S(1)} all-to-all(bf16[64,4,128]{2,1,0:T(4,128)(2,1)S(1)} %bitcast.7), channel_id=1, replica_groups=mesh['chan'=64,'tm'=8] {'chan'}, dimensions={0} | all-to-all | bytes 131072 | tf_op jit(solution)/shard_map/all_to_all | solution.py:152
  30.4 0.0 copy-start.1
  30.4 0.0 copy-done
  30.4 0.7 %copy-done.1 = s32[8]{0:T(128)S(1)} copy-done((s32[8]{0:T(128)S(1)}, s32[8]{0:T(128)}, u32[]{:S(2)}) %copy-start.1) | copy-done | bytes 56
  31.0 2.0 %trials.1 = bf16[8,32,256]{2,1,0:T(8,128)(2,1)} custom-call(s32[8]{0:T(128)S(1)} %copy-done.1, bf16[256,128]{1,0:T(8,128)(2,1)S(1)} %bitcast.6, s32[32,64]{1,0:T(8,128)S(1)} %bitcast.8), custom_call_target="tpu_custom_call" | custom-call | tf_op jit(solution)/shard_map/trials/pallas_call | solution.py:153
Async XLA Ops:
  0.0 7.4 %collective-permute-start = (bf16[256,256]{1,0:T(8,128)(2,1)}, bf16[256,256]{1,0:T(8,128)(2,1)S(1)}, u32[]{:S(2)}, u32[]{:S(2)}) collective-permute-start(bf16[256,256]{1,0:T(8,128)(2,1)} %spectra_ref.1), channel_id=1, source_target_pairs={{1,0},{2,1},{3,2},{4,3},{5,4},{6,5},{7,6},{9,8},{10,9},{11,10},{12... | collective-permute-start | bytes 393224 | tf_op jit(solution)/shard_map/ppermute | solution.py:128
  1.3 0.9 %copy-start.2 = (bf16[256,256]{1,0:T(8,128)(2,1)S(1)}, bf16[256,256]{1,0:T(8,128)(2,1)}, u32[]{:S(2)}) copy-start(bf16[256,256]{1,0:T(8,128)(2,1)} %spectra_ref.1) | copy-start | bytes 393220
  2.2 0.8 %copy-start.3 = (s32[256,64]{0,1:T(8,128)S(1)}, s32[256,64]{0,1:T(8,128)}, u32[]{:S(2)}) copy-start(s32[256,64]{0,1:T(8,128)} %param.5) | copy-start | bytes 196612
  8.6 21.8 %copy-start = (s32[64,1,32]{0,2,1:T(8,128)S(1)}, s32[64,1,32]{0,2,1:T(8,128)}, u32[]{:S(2)}) copy-start(s32[64,1,32]{0,2,1:T(8,128)} %param.6) | copy-start | bytes 24580
  30.4 0.7 %copy-start.1 = (s32[8]{0:T(128)S(1)}, s32[8]{0:T(128)}, u32[]{:S(2)}) copy-start(s32[8]{0:T(128)} %widths_ref.1) | copy-start | bytes 100

commit v2 on v1

--- a/solution.py
+++ b/solution.py
@@ -46,7 +46,30 @@
             acc_ref[...] += part
 
 
-def own_kernel(spectra_ref, delay_ref, out_ref, acc_ref):
+def own_kernel(
+    spectra_hbm, delay_hbm, fine_hbm, widths_hbm,
+    out_ref, selector_ref, triangle_ref, turn_ref, scale_ref,
+    spectra_ref, delay_ref, fine_ref, widths_ref, acc_ref, sems,
+):
+    copies = [
+        pltpu.make_async_copy(source, target, sems.at[i])
+        for i, (source, target) in enumerate(
+            [
+                (spectra_hbm, spectra_ref),
+                (delay_hbm, delay_ref),
+                (fine_hbm, fine_ref),
+                (widths_hbm, widths_ref),
+            ]
+        )
+    ]
+    for copy in copies:
+        copy.start()
+    length = triangle_ref.shape[0]
+    before = lax.broadcasted_iota(jnp.int32, (length, length), 0)
+    after = lax.broadcasted_iota(jnp.int32, (length, length), 1)
+    triangle_ref[...] = jnp.where(before < after, 1.0, 0.0).astype(jnp.bfloat16)
+    for copy in copies:
+        copy.wait()
     nblk, steps = out_ref.shape
     delay = delay_ref[...].astype(jnp.bfloat16)
     level_sums(delay, spectra_ref[...], shift_left, acc_ref)
@@ -54,6 +77,14 @@
     for q in range(1, Q1):
         total = total + shift_left(acc_ref[nblk * q : nblk * (q + 1), :], R1 * q)
     out_ref[...] = total
+    fine = fine_ref[...]
+    fine = jnp.concatenate([fine - r for r in range(R2)], axis=1).astype(jnp.bfloat16)
+    selector_ref[...] = jnp.concatenate([one_hot(fine, float(R2 * q)) for q in range(Q2)], axis=0)
+    lane = lax.broadcasted_iota(jnp.int32, (1, LANES), 1)
+    for index in range(turn_ref.shape[0]):
+        width = jnp.full((1, LANES), widths_ref[index])
+        turn_ref[index : index + 1, :] = (lane + width) & (LANES - 1)
+        scale_ref[index : index + 1, :] = 1.0 / jnp.sqrt(width.astype(jnp.float32))
 
 
 def next_kernel(own_ref, spectra_ref, delay_ref, out_ref, acc_ref, rows_ref):
@@ -74,40 +105,36 @@
     out_ref[...] = rows_ref[...].astype(jnp.bfloat16)
 
 
-def trial_kernel(widths_ref, sub_ref, delay_ref, out_ref, rows_ref):
-    trials, nsub = delay_ref.shape
+def trial_kernel(sub_ref, selector_ref, triangle_ref, turn_ref, scale_ref, out_ref, rows_ref):
+    trials = out_ref.shape[1]
+    nsub = sub_ref.shape[0] // CHUNKS
     rows_ref[...] = sub_ref[...].astype(jnp.float32)
     sub = jnp.concatenate(
         [rows_ref[pl.ds(m, nsub, stride=CHUNKS), :] for m in range(CHUNKS)], axis=1
     ).astype(jnp.bfloat16)
     shifted = jnp.concatenate([shift_left(sub, r) for r in range(R2)], axis=0)
-    delay = delay_ref[...]
-    delay = jnp.concatenate([delay - r for r in range(R2)], axis=1).astype(jnp.bfloat16)
-    selector = jnp.concatenate([one_hot(delay, float(R2 * q)) for q in range(Q2)], axis=0)
-    parts = jnp.dot(selector, shifted, preferred_element_type=jnp.float32)
+    parts = jnp.dot(selector_ref[...], shifted, preferred_element_type=jnp.float32)
     series = parts[:trials]
     for q in range(1, Q2):
         series = series + shift_left(parts[trials * q : trials * (q + 1)], R2 * q)
-    length = 3 * LANES
-    series = series[:, :length] * (1.0 / math.sqrt(CHANNELS))
+    series = series[:, : triangle_ref.shape[0]] * (1.0 / math.sqrt(CHANNELS))
     high = series.astype(jnp.bfloat16)
     rest = series - high.astype(jnp.float32)
     middle = rest.astype(jnp.bfloat16)
     low = (rest - middle.astype(jnp.float32)).astype(jnp.bfloat16)
-    before = lax.broadcasted_iota(jnp.int32, (length, length), 0)
-    after = lax.broadcasted_iota(jnp.int32, (length, length), 1)
-    triangle = jnp.where(before < after, 1.0, 0.0).astype(jnp.bfloat16)
     sums = jnp.dot(
-        jnp.concatenate([high, middle, low], axis=0), triangle, preferred_element_type=jnp.float32
+        jnp.concatenate([high, middle, low], axis=0),
+        triangle_ref[...],
+        preferred_element_type=jnp.float32,
     )
     prefix = sums[:trials] + (sums[trials : 2 * trials] + sums[2 * trials :])
     columns = [prefix[:, LANES * m : LANES * (m + 1)] for m in range(3)]
     lane = lax.broadcasted_iota(jnp.int32, (trials, LANES), 1)
     for index in range(out_ref.shape[0]):
-        width = widths_ref[index]
-        turned = [pltpu.roll(column, LANES - width, 1) for column in columns]
-        scale = 1.0 / jnp.sqrt(jnp.full((trials, LANES), width.astype(jnp.float32)))
-        inside = lane < LANES - width
+        turn = jnp.broadcast_to(turn_ref[index : index + 1, :], (trials, LANES))
+        scale = jnp.broadcast_to(scale_ref[index : index + 1, :], (trials, LANES))
+        turned = [jnp.take_along_axis(column, turn, axis=1) for column in columns]
+        inside = turn > lane
         for m in range(2):
             upper = jnp.where(inside, turned[m], turned[m + 1])
             out_ref[index, :, LANES * m : LANES * (m + 1)] = (
@@ -116,7 +143,7 @@
 
 
 VMEM = pl.BlockSpec(memory_space=pltpu.VMEM)
-SMEM = pl.BlockSpec(memory_space=pltpu.SMEM)
+ANY = pl.BlockSpec(memory_space=pl.ANY)
 PARAMS = pltpu.CompilerParams(vmem_limit_bytes=16 * 1024 * 1024)
 
 
@@ -124,21 +151,37 @@
     channels, steps = spectra.shape
     nblk = coarse_delay.shape[1]
     nsub, _, trials = fine_delay.shape
-    count = lax.axis_size("tm")
-    following = lax.ppermute(spectra, "tm", [(z + 1, z) for z in range(count - 1)])
+    blocks = lax.axis_size("tm")
+    following = lax.ppermute(spectra, "tm", [(z + 1, z) for z in range(blocks - 1)])
     by_block = coarse_delay.T
     sums = pltpu.VMEM((Q1 * nblk, steps), jnp.float32)
     flops = 2 * (D1MAX + 1) * nblk * channels * steps
-    own = pl.pallas_call(
+    fine = fine_delay.reshape(nsub, trials).T
+    count = widths.shape[0]
+    length = steps + WMAX
+    own, selector, triangle, turn, scale = pl.pallas_call(
         own_kernel,
-        out_shape=jax.ShapeDtypeStruct((nblk, steps), jnp.float32),
-        in_specs=[VMEM] * 2,
-        out_specs=VMEM,
-        scratch_shapes=[sums],
+        out_shape=[
+            jax.ShapeDtypeStruct((nblk, steps), jnp.float32),
+            jax.ShapeDtypeStruct((Q2 * trials, R2 * nsub), jnp.bfloat16),
+            jax.ShapeDtypeStruct((length, length), jnp.bfloat16),
+            jax.ShapeDtypeStruct((count, LANES), jnp.int32),
+            jax.ShapeDtypeStruct((count, LANES), jnp.float32),
+        ],
+        in_specs=[ANY] * 4,
+        out_specs=[VMEM] * 5,
+        scratch_shapes=[
+            pltpu.VMEM(spectra.shape, spectra.dtype),
+            pltpu.VMEM(by_block.shape, by_block.dtype),
+            pltpu.VMEM(fine.shape, fine.dtype),
+            pltpu.SMEM(widths.shape, widths.dtype),
+            sums,
+            pltpu.SemaphoreType.DMA((4,)),
+        ],
         compiler_params=PARAMS,
         cost_estimate=pl.CostEstimate(flops=flops, bytes_accessed=1 << 20, transcendentals=0),
         name="own_sums",
-    )(spectra, by_block)
+    )(spectra, by_block, fine, widths)
     subbands = pl.pallas_call(
         next_kernel,
         out_shape=jax.ShapeDtypeStruct((nblk * CHUNKS, LANES), jnp.bfloat16),
@@ -152,13 +195,13 @@
     received = lax.all_to_all(subbands, "chan", split_axis=0, concat_axis=0, tiled=True)
     return pl.pallas_call(
         trial_kernel,
-        out_shape=jax.ShapeDtypeStruct((widths.shape[0], trials, steps), jnp.bfloat16),
-        in_specs=[SMEM, VMEM, VMEM],
+        out_shape=jax.ShapeDtypeStruct((count, trials, steps), jnp.bfloat16),
+        in_specs=[VMEM] * 5,
         out_specs=VMEM,
         scratch_shapes=[pltpu.VMEM((nsub * CHUNKS, LANES), jnp.float32)],
         compiler_params=PARAMS,
         name="trials",
-    )(widths, received, fine_delay.reshape(nsub, trials).T)
+    )(received, selector, triangle, turn, scale)
 
 
 def solution(mesh):

time: 33.6 us -> 32.6 us (0.970)
  waiting for transfers between devices: 3.24 us -> 1.04 us
  local copies, waits for them, and re-layouts: 2.4 us -> 3.11 us
  Pallas kernels: 4.24 us -> 4.64 us
    ppermute x1, waiting for transfers between devices: 3.24 us -> 1.04 us  [per_device(): lax.ppermute(spectra, 'tm', [(z + 1, z) for z in range(blocks - 1)])]
    unnamed x8, local copies, waits for them, and re-layouts: 2.4 us -> 3.11 us
    pallas_call x2, Pallas kernels: 3.07 us -> 3.47 us  [the longest x1 1.92 us: per_device(): pl.pallas_call(own_kernel, out_shape=[jax.ShapeDtypeStruct((nblk, steps),...]
  transfers between devices with their start and end apart: 1 -> 1, of which waited for: 1 -> 1; matrix products, arithmetic and copies ran while one was open for 0% -> 0% of each run, Pallas kernels for 3% -> 6%
where the time goes in v2:
time: 32.6 us; the launch traced here: 31.9 us
  blocking collectives  21.8 us (67%)
  Pallas kernels  4.64 us (14%)
  local copies, waits for them, and re-layouts  3.11 us (10%)
  starting transfers between devices  1.28 us (4%)
  waiting for transfers between devices  1.04 us (3%)
    all_to_all x1, blocking collectives, per_device(): lax.all_to_all(subbands, 'chan', split_axis=0, concat_axis=0, tiled=True)  21.8 us
    unnamed x8, local copies, waits for them, and re-layouts  3.11 us
    pallas_call x1, Pallas kernels, per_device(): pl.pallas_call(own_kernel, out_shape=[jax.ShapeDtypeStruct((nblk, steps),...  1.92 us
    pallas_call x1, Pallas kernels, per_device(): pl.pallas_call(trial_kernel, out_shape=jax.ShapeDtypeStruct((count, trial...  1.55 us
    ppermute x1, starting transfers between devices, per_device(): lax.ppermute(spectra, 'tm', [(z + 1, z) for z in range(blocks - 1)])  1.28 us
    pallas_call x1, Pallas kernels, per_device(): pl.pallas_call(next_kernel, out_shape=jax.ShapeDtypeStruct((nblk * CHUNKS...  1.17 us
    ppermute x1, waiting for transfers between devices, per_device(): lax.ppermute(spectra, 'tm', [(z + 1, z) for z in range(blocks - 1)])  1.04 us
  transfers between devices with their start and end apart: 1, of which 1 were waited for; matrix products, arithmetic and copies ran while one was open for 0% of the time, Pallas kernels for 6%

profile of v2, /device:TPU:1, one launch (start us, length us, event | category | flops | bytes accessed | tf_op | source)
XLA Modules:
  0.0 31.9 jit_solution(4399296305202347890)
XLA Ops:
  0.0 1.3 %collective-permute-start = (bf16[256,256]{1,0:T(8,128)(2,1)}, bf16[256,256]{1,0:T(8,128)(2,1)S(1)}, u32[]{:S(2)}, u32[]{:S(2)}) collective-permute-start(bf16[256,256]{1,0:T(8,128)(2,1)} %spectra_hbm.1), channel_id=1, source_target_pairs={{1,0},{2,1},{3,2},{4,3},{5,4},{6,5},{7,6},{9,8},{10,9},{11,10},{12... | collective-permute-start | bytes 393224 | tf_op jit(solution)/shard_map/ppermute | solution.py:155
  1.3 0.0 copy-start.3
  1.3 0.6 %copy-done.3 = s32[8]{0:T(128)S(1)} copy-done((s32[8]{0:T(128)S(1)}, s32[8]{0:T(128)}, u32[]{:S(2)}) %copy-start.3) | copy-done | bytes 56
  1.9 0.0 copy-start
  1.9 0.9 %copy-done = bf16[256,256]{1,0:T(8,128)(2,1)S(1)} copy-done((bf16[256,256]{1,0:T(8,128)(2,1)S(1)}, bf16[256,256]{1,0:T(8,128)(2,1)}, u32[]{:S(2)}) %copy-start) | copy-done | bytes 131096
  2.9 0.0 copy-start.1
  2.9 0.8 %copy-done.1 = s32[256,64]{0,1:T(8,128)S(1)} copy-done((s32[256,64]{0,1:T(8,128)S(1)}, s32[256,64]{0,1:T(8,128)}, u32[]{:S(2)}) %copy-start.1) | copy-done | bytes 65560
  3.7 0.0 copy-start.2
  3.7 0.7 %copy-done.2 = s32[64,1,32]{0,2,1:T(8,128)S(1)} copy-done((s32[64,1,32]{0,2,1:T(8,128)S(1)}, s32[64,1,32]{0,2,1:T(8,128)}, u32[]{:S(2)}) %copy-start.2) | copy-done | bytes 8216
  4.4 1.9 %own_sums.1 = (f32[64,256]{1,0:T(8,128)S(1)}, bf16[256,256]{1,0:T(8,128)(2,1)S(1)}, bf16[384,384]{1,0:T(8,128)(2,1)S(1)}, s32[8,128]{1,0:T(8,128)S(1)}, f32[8,128]{1,0:T(8,128)S(1)}) custom-call(bf16[256,256]{1,0:T(8,128)(2,1)S(1)} %copy-done, s32[64,256]{1,0:T(8,128)S(1)} %bitcast.8, s32[32,64]{1,0:T(8,128)S(1)} %bitcast.10, s32[8]{0:T(128)S(1)} %copy-done.3), custom_call_target="tpu_custom_call" | custom-call | flops 805306368 | bytes 1048576 | tf_op jit(solution)/shard_map/own_sums/pallas_call | solution.py:162
  6.3 1.0 %collective-permute-done.spectra_ref = bf16[256,256]{1,0:T(8,128)(2,1)S(1)} collective-permute-done((bf16[256,256]{1,0:T(8,128)(2,1)}, bf16[256,256]{1,0:T(8,128)(2,1)S(1)}, u32[]{:S(2)}, u32[]{:S(2)}) %collective-permute-start) | collective-permute-done | bytes 131104 | tf_op jit(solution)/shard_map/ppermute | solution.py:155
  7.4 1.2 %next_sums.1 = bf16[256,128]{1,0:T(8,128)(2,1)S(1)} custom-call(f32[64,256]{1,0:T(8,128)S(1)} %get-tuple-element.10.own_ref, bf16[256,256]{1,0:T(8,128)(2,1)S(1)} %collective-permute-done.spectra_ref, s32[64,256]{1,0:T(8,128)S(1)} %bitcast.9), custom_call_target="tpu_custom_call" | custom-call | flops 805306368 | bytes 1048576 | tf_op jit(solution)/shard_map/next_sums/pallas_call | solution.py:185
  8.6 21.8 %all_to_all.11 = bf16[64,4,128]{2,1,0:T(4,128)(2,1)S(1)} all-to-all(bf16[64,4,128]{2,1,0:T(4,128)(2,1)S(1)} %bitcast.7), channel_id=1, replica_groups=mesh['chan'=64,'tm'=8] {'chan'}, dimensions={0} | all-to-all | bytes 131072 | tf_op jit(solution)/shard_map/all_to_all | solution.py:195
  30.4 1.6 %trials.1 = bf16[8,32,256]{2,1,0:T(8,128)(2,1)} custom-call(bf16[256,128]{1,0:T(8,128)(2,1)S(1)} %bitcast.6, bf16[256,256]{1,0:T(8,128)(2,1)S(1)} %get-tuple-element.11.selector_ref, bf16[384,384]{1,0:T(8,128)(2,1)S(1)} %get-tuple-element.12.triangle_ref, s32[8,128]{1,0:T(8,128)S(1)} %get-tuple-element.13.turn_ref, f32[8,128]{1,0:T(8,128)S(1)} %get-tuple-element.14.scale_ref), custom_call_target="tpu_custom_call" | custom-call | tf_op jit(solution)/shard_map/trials/pallas_call | solution.py:196
Async XLA Ops:
  0.0 7.4 %collective-permute-start = (bf16[256,256]{1,0:T(8,128)(2,1)}, bf16[256,256]{1,0:T(8,128)(2,1)S(1)}, u32[]{:S(2)}, u32[]{:S(2)}) collective-permute-start(bf16[256,256]{1,0:T(8,128)(2,1)} %spectra_hbm.1), channel_id=1, source_target_pairs={{1,0},{2,1},{3,2},{4,3},{5,4},{6,5},{7,6},{9,8},{10,9},{11,10},{12... | collective-permute-start | bytes 393224 | tf_op jit(solution)/shard_map/ppermute | solution.py:155
  1.3 0.7 %copy-start.3 = (s32[8]{0:T(128)S(1)}, s32[8]{0:T(128)}, u32[]{:S(2)}) copy-start(s32[8]{0:T(128)} %widths_hbm.1) | copy-start | bytes 100
  1.9 0.9 %copy-start = (bf16[256,256]{1,0:T(8,128)(2,1)S(1)}, bf16[256,256]{1,0:T(8,128)(2,1)}, u32[]{:S(2)}) copy-start(bf16[256,256]{1,0:T(8,128)(2,1)} %spectra_hbm.1) | copy-start | bytes 393220
  2.9 0.8 %copy-start.1 = (s32[256,64]{0,1:T(8,128)S(1)}, s32[256,64]{0,1:T(8,128)}, u32[]{:S(2)}) copy-start(s32[256,64]{0,1:T(8,128)} %param.5) | copy-start | bytes 196612
  3.7 0.7 %copy-start.2 = (s32[64,1,32]{0,2,1:T(8,128)S(1)}, s32[64,1,32]{0,2,1:T(8,128)}, u32[]{:S(2)}) copy-start(s32[64,1,32]{0,2,1:T(8,128)} %param.6) | copy-start | bytes 24580

commit v3 on v2

--- a/solution.py
+++ b/solution.py
@@ -13,6 +13,7 @@
 D2MAX = 31
 WMAX = 128
 LANES = 128
+MARGIN = D1MAX + 1
 R1 = 8
 Q1 = (D1MAX + 1) // R1
 R2 = 4
@@ -26,41 +27,58 @@
     return jnp.concatenate([x[:, by:], jnp.zeros((x.shape[0], by), x.dtype)], axis=1)
 
 
-def shift_right(x, by):
+def turn_left(x, by):
     if by == 0:
         return x
-    return jnp.concatenate([jnp.zeros((x.shape[0], by), x.dtype), x[:, :-by]], axis=1)
+    return jnp.concatenate([x[:, by:], x[:, :by]], axis=1)
 
 
 def one_hot(delay, level):
     return jnp.where(delay == level, jnp.ones((), jnp.bfloat16), jnp.zeros((), jnp.bfloat16))
 
 
-def level_sums(delay, spectra, shift, acc_ref):
+def own_kernel(
+    spectra_hbm, delay_hbm, out_ref, sent_ref,
+    spectra_ref, delay_ref, acc_ref, before_ref, sems,
+):
+    copies = [
+        pltpu.make_async_copy(spectra_hbm, spectra_ref, sems.at[0]),
+        pltpu.make_async_copy(delay_hbm, delay_ref, sems.at[1]),
+    ]
+    for copy in copies:
+        copy.start()
+    for copy in copies:
+        copy.wait()
+    nblk, steps = out_ref.shape
+    last = steps - LANES
+    spectra = spectra_ref[...]
+    delay = delay_ref[...].astype(jnp.bfloat16)
+    lane = lax.broadcasted_iota(jnp.int32, (1, LANES), 1)
     for r in range(R1):
         selector = jnp.concatenate([one_hot(delay, float(R1 * q + r)) for q in range(Q1)], axis=0)
-        part = jnp.dot(selector, shift(spectra, r), preferred_element_type=jnp.float32)
+        part = jnp.dot(selector, turn_left(spectra, r), preferred_element_type=jnp.float32)
         if r == 0:
             acc_ref[...] = part
+            before_ref[...] = jnp.zeros(before_ref.shape, jnp.float32)
         else:
-            acc_ref[...] += part
-
-
-def own_kernel(
-    spectra_hbm, delay_hbm, fine_hbm, widths_hbm,
-    out_ref, selector_ref, triangle_ref, turn_ref, scale_ref,
-    spectra_ref, delay_ref, fine_ref, widths_ref, acc_ref, sems,
-):
+            acc_ref[:, :last] += part[:, :last]
+            over = lane >= LANES - r
+            acc_ref[:, last:] += jnp.where(over, 0.0, part[:, last:])
+            before_ref[...] += jnp.where(over, part[:, last:], 0.0)
+    total = jnp.zeros((nblk, LANES + steps), jnp.float32)
+    for q in range(Q1):
+        rows = slice(nblk * q, nblk * (q + 1))
+        total = total + shift_left(
+            jnp.concatenate([before_ref[rows, :], acc_ref[rows, :]], axis=1), R1 * q
+        )
+    out_ref[...] = total[:, LANES:]
+    sent_ref[...] = total[:, LANES - MARGIN : LANES - MARGIN + steps]
+
+
+def ready_kernel(fine_hbm, widths_hbm, selector_ref, triangle_ref, turn_ref, scale_ref, fine_ref, widths_ref, sems):
     copies = [
-        pltpu.make_async_copy(source, target, sems.at[i])
-        for i, (source, target) in enumerate(
-            [
-                (spectra_hbm, spectra_ref),
-                (delay_hbm, delay_ref),
-                (fine_hbm, fine_ref),
-                (widths_hbm, widths_ref),
-            ]
-        )
+        pltpu.make_async_copy(fine_hbm, fine_ref, sems.at[0]),
+        pltpu.make_async_copy(widths_hbm, widths_ref, sems.at[1]),
     ]
     for copy in copies:
         copy.start()
@@ -70,13 +88,6 @@
     triangle_ref[...] = jnp.where(before < after, 1.0, 0.0).astype(jnp.bfloat16)
     for copy in copies:
         copy.wait()
-    nblk, steps = out_ref.shape
-    delay = delay_ref[...].astype(jnp.bfloat16)
-    level_sums(delay, spectra_ref[...], shift_left, acc_ref)
-    total = acc_ref[0:nblk, :]
-    for q in range(1, Q1):
-        total = total + shift_left(acc_ref[nblk * q : nblk * (q + 1), :], R1 * q)
-    out_ref[...] = total
     fine = fine_ref[...]
     fine = jnp.concatenate([fine - r for r in range(R2)], axis=1).astype(jnp.bfloat16)
     selector_ref[...] = jnp.concatenate([one_hot(fine, float(R2 * q)) for q in range(Q2)], axis=0)
@@ -87,17 +98,17 @@
         scale_ref[index : index + 1, :] = 1.0 / jnp.sqrt(width.astype(jnp.float32))
 
 
-def next_kernel(own_ref, spectra_ref, delay_ref, out_ref, acc_ref, rows_ref):
+def join_kernel(own_ref, next_ref, out_ref, rows_ref):
     nblk, steps = own_ref.shape
-    delay = delay_ref[...].astype(jnp.bfloat16)
-    level_sums(delay, spectra_ref[...], lambda x, r: shift_right(x, R1 - r), acc_ref)
-    total = jnp.zeros((nblk, steps + LANES), jnp.float32)
-    for q in range(Q1):
-        left = LANES - R1 * (q + 1)
-        pieces = [acc_ref[nblk * q : nblk * (q + 1), :], jnp.zeros((nblk, LANES - left), jnp.float32)]
-        if left:
-            pieces = [jnp.zeros((nblk, left), jnp.float32)] + pieces
-        total = total + jnp.concatenate(pieces, axis=1)
+    left = steps - MARGIN - LANES
+    total = jnp.concatenate(
+        [
+            jnp.zeros((nblk, left), jnp.float32),
+            next_ref[...],
+            jnp.zeros((nblk, 3 * LANES - left - steps), jnp.float32),
+        ],
+        axis=1,
+    )
     rows_ref[pl.ds(0, nblk, stride=CHUNKS), :] = own_ref[:, :LANES]
     rows_ref[pl.ds(1, nblk, stride=CHUNKS), :] = own_ref[:, LANES:] + total[:, :LANES]
     rows_ref[pl.ds(2, nblk, stride=CHUNKS), :] = total[:, LANES : 2 * LANES]
@@ -143,7 +154,7 @@
 
 
 VMEM = pl.BlockSpec(memory_space=pltpu.VMEM)
-ANY = pl.BlockSpec(memory_space=pl.ANY)
+HBM = pl.BlockSpec(memory_space=pltpu.HBM)
 PARAMS = pltpu.CompilerParams(vmem_limit_bytes=16 * 1024 * 1024)
 
 
@@ -151,47 +162,55 @@
     channels, steps = spectra.shape
     nblk = coarse_delay.shape[1]
     nsub, _, trials = fine_delay.shape
-    blocks = lax.axis_size("tm")
-    following = lax.ppermute(spectra, "tm", [(z + 1, z) for z in range(blocks - 1)])
-    by_block = coarse_delay.T
-    sums = pltpu.VMEM((Q1 * nblk, steps), jnp.float32)
-    flops = 2 * (D1MAX + 1) * nblk * channels * steps
-    fine = fine_delay.reshape(nsub, trials).T
     count = widths.shape[0]
     length = steps + WMAX
-    own, selector, triangle, turn, scale = pl.pallas_call(
+    by_block = coarse_delay.T
+    fine = fine_delay.reshape(nsub, trials).T
+    own, sent = pl.pallas_call(
         own_kernel,
+        out_shape=[jax.ShapeDtypeStruct((nblk, steps), jnp.float32)] * 2,
+        in_specs=[HBM] * 2,
+        out_specs=[VMEM] * 2,
+        scratch_shapes=[
+            pltpu.VMEM(spectra.shape, spectra.dtype),
+            pltpu.VMEM(by_block.shape, by_block.dtype),
+            pltpu.VMEM((Q1 * nblk, steps), jnp.float32),
+            pltpu.VMEM((Q1 * nblk, LANES), jnp.float32),
+            pltpu.SemaphoreType.DMA((2,)),
+        ],
+        compiler_params=PARAMS,
+        name="own_sums",
+    )(*(pltpu.with_memory_space_constraint(x, pltpu.HBM) for x in (spectra, by_block)))
+    blocks = lax.axis_size("tm")
+    following = lax.ppermute(sent, "tm", [(z + 1, z) for z in range(blocks - 1)])
+    selector, triangle, turn, scale = pl.pallas_call(
+        ready_kernel,
         out_shape=[
-            jax.ShapeDtypeStruct((nblk, steps), jnp.float32),
             jax.ShapeDtypeStruct((Q2 * trials, R2 * nsub), jnp.bfloat16),
             jax.ShapeDtypeStruct((length, length), jnp.bfloat16),
             jax.ShapeDtypeStruct((count, LANES), jnp.int32),
             jax.ShapeDtypeStruct((count, LANES), jnp.float32),
         ],
-        in_specs=[ANY] * 4,
-        out_specs=[VMEM] * 5,
+        in_specs=[HBM] * 2,
+        out_specs=[VMEM] * 4,
         scratch_shapes=[
-            pltpu.VMEM(spectra.shape, spectra.dtype),
-            pltpu.VMEM(by_block.shape, by_block.dtype),
             pltpu.VMEM(fine.shape, fine.dtype),
             pltpu.SMEM(widths.shape, widths.dtype),
-            sums,
-            pltpu.SemaphoreType.DMA((4,)),
-        ],
-        compiler_params=PARAMS,
-        cost_estimate=pl.CostEstimate(flops=flops, bytes_accessed=1 << 20, transcendentals=0),
-        name="own_sums",
-    )(spectra, by_block, fine, widths)
+            pltpu.SemaphoreType.DMA((2,)),
+        ],
+        compiler_params=PARAMS,
+        cost_estimate=pl.CostEstimate(flops=1 << 30, bytes_accessed=1 << 20, transcendentals=0),
+        name="ready",
+    )(*(pltpu.with_memory_space_constraint(x, pltpu.HBM) for x in (fine, widths)))
     subbands = pl.pallas_call(
-        next_kernel,
+        join_kernel,
         out_shape=jax.ShapeDtypeStruct((nblk * CHUNKS, LANES), jnp.bfloat16),
-        in_specs=[VMEM] * 3,
+        in_specs=[VMEM] * 2,
         out_specs=VMEM,
-        scratch_shapes=[sums, pltpu.VMEM((nblk * CHUNKS, LANES), jnp.float32)],
-        compiler_params=PARAMS,
-        cost_estimate=pl.CostEstimate(flops=flops, bytes_accessed=1 << 20, transcendentals=0),
-        name="next_sums",
-    )(own, following, by_block)
+        scratch_shapes=[pltpu.VMEM((nblk * CHUNKS, LANES), jnp.float32)],
+        compiler_params=PARAMS,
+        name="join",
+    )(own, following)
     received = lax.all_to_all(subbands, "chan", split_axis=0, concat_axis=0, tiled=True)
     return pl.pallas_call(
         trial_kernel,

time: 32.6 us -> 33.1 us (1.015)
  blocking collectives: 21.8 us -> 0 us
  waiting for transfers between devices: 1.04 us -> 14.1 us
  starting transfers between devices: 1.28 us -> 13 us
  local copies, waits for them, and re-layouts: 3.11 us -> 0 us
  Pallas kernels: 4.64 us -> 5.42 us
    all_to_all x1 -> x0, blocking collectives: 21.8 us -> none  [per_device(): lax.all_to_all(subbands, 'chan', split_axis=0, concat_axis=0, tiled=True)]
    all_to_all x0 -> x1, starting transfers between devices: none -> 11.7 us  [per_device(): lax.all_to_all(subbands, 'chan', split_axis=0, concat_axis=0, tiled=True)]
    all_to_all x0 -> x1, waiting for transfers between devices: none -> 8.87 us  [per_device(): lax.all_to_all(subbands, 'chan', split_axis=0, concat_axis=0, tiled=True)]
    ppermute x1, waiting for transfers between devices: 1.04 us -> 5.18 us  [per_device(): lax.ppermute(sent, 'tm', [(z + 1, z) for z in range(blocks - 1)])]
    unnamed x8 -> x0, local copies, waits for them, and re-layouts: 3.11 us -> none
    pallas_call x1 -> x2, Pallas kernels: 1.17 us -> 1.63 us  [the longest x1 0.91 us: per_device(): pl.pallas_call(ready_kernel, out_shape=[jax.ShapeDtypeStruct((Q2 * trials...]
  transfers between devices with their start and end apart: 1 -> 2, of which waited for: 1 -> 2; matrix products, arithmetic and copies ran while one was open for 0% -> 0% of each run, Pallas kernels for 6% -> 3%
where the time goes in v3:
time: 33.1 us; the launch traced here: 32.5 us
  waiting for transfers between devices  14.1 us (43%)
  starting transfers between devices  13 us (39%)
  Pallas kernels  5.42 us (16%)
    all_to_all x1, starting transfers between devices, per_device(): lax.all_to_all(subbands, 'chan', split_axis=0, concat_axis=0, tiled=True)  11.7 us
    all_to_all x1, waiting for transfers between devices, per_device(): lax.all_to_all(subbands, 'chan', split_axis=0, concat_axis=0, tiled=True)  8.87 us
    ppermute x1, waiting for transfers between devices, per_device(): lax.ppermute(sent, 'tm', [(z + 1, z) for z in range(blocks - 1)])  5.18 us
    pallas_call x1, Pallas kernels, per_device(): pl.pallas_call(own_kernel, out_shape=[jax.ShapeDtypeStruct((nblk, steps),...  2.24 us
    pallas_call x1, Pallas kernels, per_device(): pl.pallas_call(trial_kernel, out_shape=jax.ShapeDtypeStruct((count, trial...  1.55 us
    ppermute x1, starting transfers between devices, per_device(): lax.ppermute(sent, 'tm', [(z + 1, z) for z in range(blocks - 1)])  1.29 us
    pallas_call x1, Pallas kernels, per_device(): pl.pallas_call(ready_kernel, out_shape=[jax.ShapeDtypeStruct((Q2 * trials...  0.91 us
    pallas_call x1, Pallas kernels, per_device(): pl.pallas_call(join_kernel, out_shape=jax.ShapeDtypeStruct((nblk * CHUNKS...  0.72 us
  transfers between devices with their start and end apart: 2, of which 2 were waited for; matrix products, arithmetic and copies ran while one was open for 0% of the time, Pallas kernels for 3%

profile of v3, /device:TPU:1, one launch (start us, length us, event | category | flops | bytes accessed | tf_op | source)
XLA Modules:
  0.0 32.5 jit_solution(17259296828920222120)
XLA Ops:
  0.0 2.2 %own_sums.1 = (f32[64,256]{1,0:T(8,128)S(1)}, f32[64,256]{1,0:T(8,128)S(1)}) custom-call(bf16[256,256]{1,0:T(8,128)(2,1)} %spectra_hbm.1, s32[64,256]{1,0:T(8,128)} %bitcast.7), custom_call_target="tpu_custom_call" | custom-call | tf_op jit(solution)/shard_map/own_sums/pallas_call | solution.py:169
  2.2 1.3 %collective-permute-start = (f32[64,256]{1,0:T(8,128)S(1)}, f32[64,256]{1,0:T(8,128)S(1)}, u32[]{:S(2)}, u32[]{:S(2)}) collective-permute-start(f32[64,256]{1,0:T(8,128)S(1)} %get-tuple-element.12), channel_id=1, source_target_pairs={{1,0},{2,1},{3,2},{4,3},{5,4},{6,5},{7,6},{9,8},{10,9},{11,10},{12... | collective-permute-start | bytes 196616 | tf_op jit(solution)/shard_map/ppermute | solution.py:185
  3.5 5.2 %collective-permute-done.next_ref = f32[64,256]{1,0:T(8,128)S(1)} collective-permute-done((f32[64,256]{1,0:T(8,128)S(1)}, f32[64,256]{1,0:T(8,128)S(1)}, u32[]{:S(2)}, u32[]{:S(2)}) %collective-permute-start) | collective-permute-done | bytes 65568 | tf_op jit(solution)/shard_map/ppermute | solution.py:185
  8.7 0.7 %join.1 = bf16[256,128]{1,0:T(8,128)(2,1)} custom-call(f32[64,256]{1,0:T(8,128)S(1)} %get-tuple-element.11.own_ref, f32[64,256]{1,0:T(8,128)S(1)} %collective-permute-done.next_ref), custom_call_target="tpu_custom_call" | custom-call | tf_op jit(solution)/shard_map/join/pallas_call | solution.py:205
  9.4 11.7 %all-to-all-start = ((bf16[64,4,128]{2,1,0:T(4,128)(2,1)}), bf16[64,4,128]{2,1,0:T(4,128)(2,1)S(1)}, u32[]{:S(2)}, u32[]{:S(2)}) async-start(bf16[64,4,128]{2,1,0:T(4,128)(2,1)} %bitcast.1), calls=%async_computation | async-start | bytes 131072 | tf_op jit(solution)/shard_map/all_to_all | solution.py:214
  21.1 0.9 %ready.1 = (bf16[256,256]{1,0:T(8,128)(2,1)S(1)}, bf16[384,384]{1,0:T(8,128)(2,1)S(1)}, s32[8,128]{1,0:T(8,128)S(1)}, f32[8,128]{1,0:T(8,128)S(1)}) custom-call(s32[32,64]{1,0:T(8,128)} %bitcast.8, s32[8]{0:T(128)} %widths_hbm.1), custom_call_target="tpu_custom_call" | custom-call | flops 1073741824 | bytes 1048576 | tf_op jit(solution)/shard_map/ready/pallas_call | solution.py:186
  22.0 8.9 %all-to-all-done = bf16[64,4,128]{2,1,0:T(4,128)(2,1)S(1)} async-done(((bf16[64,4,128]{2,1,0:T(4,128)(2,1)}), bf16[64,4,128]{2,1,0:T(4,128)(2,1)S(1)}, u32[]{:S(2)}, u32[]{:S(2)}) %all-to-all-start) | async-done | bytes 65568 | tf_op jit(solution)/shard_map/all_to_all | solution.py:214
  30.9 1.6 %trials.1 = bf16[8,32,256]{2,1,0:T(8,128)(2,1)} custom-call(bf16[256,128]{1,0:T(8,128)(2,1)S(1)} %bitcast.6, bf16[256,256]{1,0:T(8,128)(2,1)S(1)} %get-tuple-element.13.selector_ref, bf16[384,384]{1,0:T(8,128)(2,1)S(1)} %get-tuple-element.14.triangle_ref, s32[8,128]{1,0:T(8,128)S(1)} %get-tuple-element.15.turn_ref, f32[8,128]{1,0:T(8,128)S(1)} %get-tuple-element.16.scale_ref), custom_call_target="tpu_custom_call" | custom-call | tf_op jit(solution)/shard_map/trials/pallas_call | solution.py:215
Async XLA Ops:
  2.2 6.5 %collective-permute-start = (f32[64,256]{1,0:T(8,128)S(1)}, f32[64,256]{1,0:T(8,128)S(1)}, u32[]{:S(2)}, u32[]{:S(2)}) collective-permute-start(f32[64,256]{1,0:T(8,128)S(1)} %get-tuple-element.12), channel_id=1, source_target_pairs={{1,0},{2,1},{3,2},{4,3},{5,4},{6,5},{7,6},{9,8},{10,9},{11,10},{12... | collective-permute-start | bytes 196616 | tf_op jit(solution)/shard_map/ppermute | solution.py:185
  9.4 21.5 %all-to-all-start = ((bf16[64,4,128]{2,1,0:T(4,128)(2,1)}), bf16[64,4,128]{2,1,0:T(4,128)(2,1)S(1)}, u32[]{:S(2)}, u32[]{:S(2)}) async-start(bf16[64,4,128]{2,1,0:T(4,128)(2,1)} %bitcast.1), calls=%async_computation | async-start | bytes 131072 | tf_op jit(solution)/shard_map/all_to_all | solution.py:214

commit v4 on v3

--- a/solution.py
+++ b/solution.py
@@ -18,6 +18,7 @@
 Q1 = (D1MAX + 1) // R1
 R2 = 4
 Q2 = (D2MAX + 1) // R2
+ROOT = 41
 CHUNKS = 4
 
 
@@ -33,11 +34,16 @@
     return jnp.concatenate([x[:, by:], x[:, :by]], axis=1)
 
 
+def from_root(x, axis):
+    first, second = jnp.split(x, [ROOT], axis=axis)
+    return jnp.concatenate([second, first], axis=axis)
+
+
 def one_hot(delay, level):
     return jnp.where(delay == level, jnp.ones((), jnp.bfloat16), jnp.zeros((), jnp.bfloat16))
 
 
-def own_kernel(
+def own_sums(
     spectra_hbm, delay_hbm, out_ref, sent_ref,
     spectra_ref, delay_ref, acc_ref, before_ref, sems,
 ):
@@ -52,7 +58,7 @@
     nblk, steps = out_ref.shape
     last = steps - LANES
     spectra = spectra_ref[...]
-    delay = delay_ref[...].astype(jnp.bfloat16)
+    delay = from_root(delay_ref[...], 0).astype(jnp.bfloat16)
     lane = lax.broadcasted_iota(jnp.int32, (1, LANES), 1)
     for r in range(R1):
         selector = jnp.concatenate([one_hot(delay, float(R1 * q + r)) for q in range(Q1)], axis=0)
@@ -72,7 +78,22 @@
             jnp.concatenate([before_ref[rows, :], acc_ref[rows, :]], axis=1), R1 * q
         )
     out_ref[...] = total[:, LANES:]
-    sent_ref[...] = total[:, LANES - MARGIN : LANES - MARGIN + steps]
+    if sent_ref is not None:
+        sent_ref[...] = total[:, LANES - MARGIN : LANES - MARGIN + steps]
+
+
+def sender_kernel(spectra_hbm, delay_hbm, out_ref, sent_ref, *scratch):
+    @pl.when(lax.axis_index("tm") > 0)
+    def _():
+        own_sums(spectra_hbm, delay_hbm, out_ref, sent_ref, *scratch)
+
+
+def first_kernel(spectra_hbm, delay_hbm, sums_ref, out_ref, *scratch):
+    del sums_ref
+
+    @pl.when(lax.axis_index("tm") == 0)
+    def _():
+        own_sums(spectra_hbm, delay_hbm, out_ref, None, *scratch)
 
 
 def ready_kernel(fine_hbm, widths_hbm, selector_ref, triangle_ref, turn_ref, scale_ref, fine_ref, widths_ref, sems):
@@ -88,7 +109,7 @@
     triangle_ref[...] = jnp.where(before < after, 1.0, 0.0).astype(jnp.bfloat16)
     for copy in copies:
         copy.wait()
-    fine = fine_ref[...]
+    fine = from_root(fine_ref[...], 1)
     fine = jnp.concatenate([fine - r for r in range(R2)], axis=1).astype(jnp.bfloat16)
     selector_ref[...] = jnp.concatenate([one_hot(fine, float(R2 * q)) for q in range(Q2)], axis=0)
     lane = lax.broadcasted_iota(jnp.int32, (1, LANES), 1)
@@ -98,7 +119,8 @@
         scale_ref[index : index + 1, :] = 1.0 / jnp.sqrt(width.astype(jnp.float32))
 
 
-def join_kernel(own_ref, next_ref, out_ref, rows_ref):
+def join_kernel(own_ref, next_ref, ready_ref, out_ref, rows_ref):
+    del ready_ref
     nblk, steps = own_ref.shape
     left = steps - MARGIN - LANES
     total = jnp.concatenate(
@@ -166,23 +188,37 @@
     length = steps + WMAX
     by_block = coarse_delay.T
     fine = fine_delay.reshape(nsub, trials).T
+    block = jax.ShapeDtypeStruct((nblk, steps), jnp.float32)
+    scratch = [
+        pltpu.VMEM(spectra.shape, spectra.dtype),
+        pltpu.VMEM(by_block.shape, by_block.dtype),
+        pltpu.VMEM((Q1 * nblk, steps), jnp.float32),
+        pltpu.VMEM((Q1 * nblk, LANES), jnp.float32),
+        pltpu.SemaphoreType.DMA((2,)),
+    ]
+    sources = [pltpu.with_memory_space_constraint(x, pltpu.HBM) for x in (spectra, by_block)]
     own, sent = pl.pallas_call(
-        own_kernel,
-        out_shape=[jax.ShapeDtypeStruct((nblk, steps), jnp.float32)] * 2,
+        sender_kernel,
+        out_shape=[block] * 2,
         in_specs=[HBM] * 2,
         out_specs=[VMEM] * 2,
-        scratch_shapes=[
-            pltpu.VMEM(spectra.shape, spectra.dtype),
-            pltpu.VMEM(by_block.shape, by_block.dtype),
-            pltpu.VMEM((Q1 * nblk, steps), jnp.float32),
-            pltpu.VMEM((Q1 * nblk, LANES), jnp.float32),
-            pltpu.SemaphoreType.DMA((2,)),
-        ],
-        compiler_params=PARAMS,
-        name="own_sums",
-    )(*(pltpu.with_memory_space_constraint(x, pltpu.HBM) for x in (spectra, by_block)))
+        scratch_shapes=scratch,
+        compiler_params=PARAMS,
+        name="sender_sums",
+    )(*sources)
     blocks = lax.axis_size("tm")
     following = lax.ppermute(sent, "tm", [(z + 1, z) for z in range(blocks - 1)])
+    own = pl.pallas_call(
+        first_kernel,
+        out_shape=block,
+        in_specs=[HBM] * 2 + [VMEM],
+        out_specs=VMEM,
+        scratch_shapes=scratch,
+        input_output_aliases={2: 0},
+        compiler_params=PARAMS,
+        cost_estimate=pl.CostEstimate(flops=1 << 30, bytes_accessed=1 << 20, transcendentals=0),
+        name="first_sums",
+    )(*sources, own)
     selector, triangle, turn, scale = pl.pallas_call(
         ready_kernel,
         out_shape=[
@@ -205,13 +241,21 @@
     subbands = pl.pallas_call(
         join_kernel,
         out_shape=jax.ShapeDtypeStruct((nblk * CHUNKS, LANES), jnp.bfloat16),
-        in_specs=[VMEM] * 2,
+        in_specs=[VMEM] * 3,
         out_specs=VMEM,
         scratch_shapes=[pltpu.VMEM((nblk * CHUNKS, LANES), jnp.float32)],
         compiler_params=PARAMS,
         name="join",
-    )(own, following)
-    received = lax.all_to_all(subbands, "chan", split_axis=0, concat_axis=0, tiled=True)
+    )(own, following, turn)
+    groups = lax.axis_size("chan")
+    received = lax.all_to_all(
+        subbands,
+        "chan",
+        split_axis=0,
+        concat_axis=0,
+        tiled=True,
+        axis_index_groups=[[(i + ROOT) % groups for i in range(groups)]],
+    )
     return pl.pallas_call(
         trial_kernel,
         out_shape=jax.ShapeDtypeStruct((count, trials, steps), jnp.bfloat16),

time: 33.1 us -> 27.3 us (0.82); the launches traced: 32.5 us -> 27 us
  blocking collectives: 0 us -> 16.7 us
  starting transfers between devices: 13 us -> 1.29 us
  waiting for transfers between devices: 14.1 us -> 4.36 us
  Pallas kernels: 5.42 us -> 4.68 us
    all_to_all x0 -> x1, blocking collectives: none -> 16.7 us  [per_device(): lax.all_to_all(subbands, 'chan', split_axis=0, concat_axis=0, tiled=True,...]
    all_to_all x1 -> x0, starting transfers between devices: 11.7 us -> none  [per_device(): lax.all_to_all(subbands, 'chan', split_axis=0, concat_axis=0, tiled=True)]
    all_to_all x1 -> x0, waiting for transfers between devices: 8.87 us -> none  [per_device(): lax.all_to_all(subbands, 'chan', split_axis=0, concat_axis=0, tiled=True)]
    ppermute x1, waiting for transfers between devices: 5.18 us -> 4.36 us  [per_device(): lax.ppermute(sent, 'tm', [(z + 1, z) for z in range(blocks - 1)])]
    pallas_call x1, Pallas kernels: 0.72 us -> 0.09 us  [per_device(): pl.pallas_call(join_kernel, out_shape=jax.ShapeDtypeStruct((nblk * CHUNKS...]
    pallas_call x1 -> x2, Pallas kernels: 2.24 us -> 2.06 us  [the longest x1 2.05 us: per_device(): pl.pallas_call(first_kernel, out_shape=block, in_specs=[HBM] * 2 + [VMEM]...]
  transfers between devices with their start and end apart: 2 -> 1, of which waited for: 2 -> 1; matrix products, arithmetic and copies ran while one was open for 0% -> 0% of each run, Pallas kernels for 3% -> 11%
where the time goes in v4:
time: 27.3 us; the launch traced here: 27 us
  blocking collectives  16.7 us (61%)
  Pallas kernels  4.68 us (17%)
  waiting for transfers between devices  4.36 us (16%)
  starting transfers between devices  1.29 us (5%)
    all_to_all x1, blocking collectives, per_device(): lax.all_to_all(subbands, 'chan', split_axis=0, concat_axis=0, tiled=True,...  16.7 us
    ppermute x1, waiting for transfers between devices, per_device(): lax.ppermute(sent, 'tm', [(z + 1, z) for z in range(blocks - 1)])  4.36 us
    pallas_call x1, Pallas kernels, per_device(): pl.pallas_call(first_kernel, out_shape=block, in_specs=[HBM] * 2 + [VMEM]...  2.05 us
    pallas_call x1, Pallas kernels, per_device(): pl.pallas_call(trial_kernel, out_shape=jax.ShapeDtypeStruct((count, trial...  1.55 us
    ppermute x1, starting transfers between devices, per_device(): lax.ppermute(sent, 'tm', [(z + 1, z) for z in range(blocks - 1)])  1.29 us
    pallas_call x1, Pallas kernels, per_device(): pl.pallas_call(ready_kernel, out_shape=[jax.ShapeDtypeStruct((Q2 * trials...  0.98 us
  transfers between devices with their start and end apart: 1, of which 1 were waited for; matrix products, arithmetic and copies ran while one was open for 0% of the time, Pallas kernels for 11%

profile of v4, /device:TPU:1, one launch (start us, length us, event | category | flops | bytes accessed | tf_op | source)
XLA Modules:
  0.0 27.0 jit_solution(18173971688414249272)
XLA Ops:
  0.0 1.3 %collective-permute-start = (f32[64,256]{1,0:T(8,128)S(1)}, f32[64,256]{1,0:T(8,128)S(1)}, u32[]{:S(2)}, u32[]{:S(2)}) collective-permute-start(f32[64,256]{1,0:T(8,128)S(1)} %get-tuple-element.12), channel_id=1, source_target_pairs={{1,0},{2,1},{3,2},{4,3},{5,4},{6,5},{7,6},{9,8},{10,9},{11,10},{12... | collective-permute-start | bytes 196616 | tf_op jit(solution)/shard_map/ppermute | solution.py:210
  1.3 2.0 %first_sums.1.own_ref = f32[64,256]{1,0:T(8,128)S(1)} custom-call(bf16[256,256]{1,0:T(8,128)(2,1)} %spectra_hbm.3, s32[64,256]{1,0:T(8,128)} %bitcast.9, f32[64,256]{1,0:T(8,128)S(1)} %get-tuple-element.11.sums_ref), custom_call_target="tpu_custom_call", output_to_operand_aliasing={{}: (2, {})} | custom-call | flops 1073741824 | bytes 1048576 | tf_op jit(solution)/shard_map/first_sums/pallas_call | solution.py:211
  3.4 1.0 %ready.1 = (bf16[256,256]{1,0:T(8,128)(2,1)S(1)}, bf16[384,384]{1,0:T(8,128)(2,1)S(1)}, s32[8,128]{1,0:T(8,128)S(1)}, f32[8,128]{1,0:T(8,128)S(1)}) custom-call(s32[32,64]{1,0:T(8,128)} %bitcast.10, s32[8]{0:T(128)} %widths_hbm.1), custom_call_target="tpu_custom_call" | custom-call | flops 1073741824 | bytes 1048576 | tf_op jit(solution)/shard_map/ready/pallas_call | solution.py:222
  4.4 4.4 %collective-permute-done.next_ref = f32[64,256]{1,0:T(8,128)S(1)} collective-permute-done((f32[64,256]{1,0:T(8,128)S(1)}, f32[64,256]{1,0:T(8,128)S(1)}, u32[]{:S(2)}, u32[]{:S(2)}) %collective-permute-start) | collective-permute-done | bytes 65568 | tf_op jit(solution)/shard_map/ppermute | solution.py:210
  8.7 0.1 join.1
  8.8 16.7 %all_to_all.11 = bf16[64,4,128]{2,1,0:T(4,128)(2,1)S(1)} all-to-all(bf16[64,4,128]{2,1,0:T(4,128)(2,1)S(1)} %bitcast.7), channel_id=1, replica_groups={{328,336,344,352,360,368,376,384,392,400,408,416,424,432,440,448,456,46..., dimensions={0} | all-to-all | bytes 131072 | tf_op jit(solution)/shard_map/all_to_all | solution.py:251
  25.5 1.6 %trials.1 = bf16[8,32,256]{2,1,0:T(8,128)(2,1)} custom-call(bf16[256,128]{1,0:T(8,128)(2,1)S(1)} %bitcast.6, bf16[256,256]{1,0:T(8,128)(2,1)S(1)} %get-tuple-element.14.selector_ref, bf16[384,384]{1,0:T(8,128)(2,1)S(1)} %get-tuple-element.15.triangle_ref, s32[8,128]{1,0:T(8,128)S(1)} %get-tuple-element.13.ready_ref.turn_ref, ...), custom_call_target="tpu_custom_call" | custom-call | tf_op jit(solution)/shard_map/trials/pallas_call | solution.py:259
  (1 shorter events, 0.0 us)
Async XLA Ops:
  0.0 8.7 %collective-permute-start = (f32[64,256]{1,0:T(8,128)S(1)}, f32[64,256]{1,0:T(8,128)S(1)}, u32[]{:S(2)}, u32[]{:S(2)}) collective-permute-start(f32[64,256]{1,0:T(8,128)S(1)} %get-tuple-element.12), channel_id=1, source_target_pairs={{1,0},{2,1},{3,2},{4,3},{5,4},{6,5},{7,6},{9,8},{10,9},{11,10},{12... | collective-permute-start | bytes 196616 | tf_op jit(solution)/shard_map/ppermute | solution.py:210

commit v5 on v4

--- a/solution.py
+++ b/solution.py
@@ -14,7 +14,7 @@
 WMAX = 128
 LANES = 128
 MARGIN = D1MAX + 1
-R1 = 8
+R1 = 16
 Q1 = (D1MAX + 1) // R1
 R2 = 4
 Q2 = (D2MAX + 1) // R2
@@ -65,21 +65,24 @@
         part = jnp.dot(selector, turn_left(spectra, r), preferred_element_type=jnp.float32)
         if r == 0:
             acc_ref[...] = part
-            before_ref[...] = jnp.zeros(before_ref.shape, jnp.float32)
+            continue
+        acc_ref[...] += part
+        over = jnp.where(lane >= LANES - r, part[:, last:], 0.0)
+        if r == 1:
+            before_ref[...] = over
         else:
-            acc_ref[:, :last] += part[:, :last]
-            over = lane >= LANES - r
-            acc_ref[:, last:] += jnp.where(over, 0.0, part[:, last:])
-            before_ref[...] += jnp.where(over, part[:, last:], 0.0)
+            before_ref[...] += over
     total = jnp.zeros((nblk, LANES + steps), jnp.float32)
     for q in range(Q1):
         rows = slice(nblk * q, nblk * (q + 1))
+        over = before_ref[rows, :]
         total = total + shift_left(
-            jnp.concatenate([before_ref[rows, :], acc_ref[rows, :]], axis=1), R1 * q
+            jnp.concatenate([over, acc_ref[rows, :last], acc_ref[rows, last:] - over], axis=1),
+            R1 * q,
         )
     out_ref[...] = total[:, LANES:]
     if sent_ref is not None:
-        sent_ref[...] = total[:, LANES - MARGIN : LANES - MARGIN + steps]
+        sent_ref[...] = total[:, LANES - MARGIN : LANES - MARGIN + steps].astype(jnp.bfloat16)
 
 
 def sender_kernel(spectra_hbm, delay_hbm, out_ref, sent_ref, *scratch):
@@ -96,27 +99,27 @@
         own_sums(spectra_hbm, delay_hbm, out_ref, None, *scratch)
 
 
-def ready_kernel(fine_hbm, widths_hbm, selector_ref, triangle_ref, turn_ref, scale_ref, fine_ref, widths_ref, sems):
+def ready_kernel(fine_hbm, widths_hbm, selector_ref, band_ref, scale_ref, fine_ref, widths_ref, sems):
     copies = [
         pltpu.make_async_copy(fine_hbm, fine_ref, sems.at[0]),
         pltpu.make_async_copy(widths_hbm, widths_ref, sems.at[1]),
     ]
     for copy in copies:
         copy.start()
-    length = triangle_ref.shape[0]
-    before = lax.broadcasted_iota(jnp.int32, (length, length), 0)
-    after = lax.broadcasted_iota(jnp.int32, (length, length), 1)
-    triangle_ref[...] = jnp.where(before < after, 1.0, 0.0).astype(jnp.bfloat16)
     for copy in copies:
         copy.wait()
     fine = from_root(fine_ref[...], 1)
     fine = jnp.concatenate([fine - r for r in range(R2)], axis=1).astype(jnp.bfloat16)
     selector_ref[...] = jnp.concatenate([one_hot(fine, float(R2 * q)) for q in range(Q2)], axis=0)
-    lane = lax.broadcasted_iota(jnp.int32, (1, LANES), 1)
-    for index in range(turn_ref.shape[0]):
-        width = jnp.full((1, LANES), widths_ref[index])
-        turn_ref[index : index + 1, :] = (lane + width) & (LANES - 1)
-        scale_ref[index : index + 1, :] = 1.0 / jnp.sqrt(width.astype(jnp.float32))
+    shape = (band_ref.shape[0], LANES)
+    ahead = lax.broadcasted_iota(jnp.int32, shape, 0) - lax.broadcasted_iota(jnp.int32, shape, 1)
+    for index in range(scale_ref.shape[0]):
+        width = widths_ref[index]
+        counts = jnp.logical_and(ahead >= 0, ahead < width)
+        band_ref[:, LANES * index : LANES * (index + 1)] = jnp.where(counts, 1.0, 0.0).astype(jnp.bfloat16)
+        scale_ref[index : index + 1, :] = 1.0 / jnp.sqrt(
+            jnp.full((1, LANES), width).astype(jnp.float32)
+        )
 
 
 def join_kernel(own_ref, next_ref, ready_ref, out_ref, rows_ref):
@@ -126,7 +129,7 @@
     total = jnp.concatenate(
         [
             jnp.zeros((nblk, left), jnp.float32),
-            next_ref[...],
+            next_ref[...].astype(jnp.float32),
             jnp.zeros((nblk, 3 * LANES - left - steps), jnp.float32),
         ],
         axis=1,
@@ -138,8 +141,8 @@
     out_ref[...] = rows_ref[...].astype(jnp.bfloat16)
 
 
-def trial_kernel(sub_ref, selector_ref, triangle_ref, turn_ref, scale_ref, out_ref, rows_ref):
-    trials = out_ref.shape[1]
+def trial_kernel(sub_ref, selector_ref, band_ref, scale_ref, out_ref, rows_ref):
+    count, trials, steps = out_ref.shape
     nsub = sub_ref.shape[0] // CHUNKS
     rows_ref[...] = sub_ref[...].astype(jnp.float32)
     sub = jnp.concatenate(
@@ -150,29 +153,23 @@
     series = parts[:trials]
     for q in range(1, Q2):
         series = series + shift_left(parts[trials * q : trials * (q + 1)], R2 * q)
-    series = series[:, : triangle_ref.shape[0]] * (1.0 / math.sqrt(CHANNELS))
+    series = series[:, : steps + WMAX] * (1.0 / math.sqrt(CHANNELS))
     high = series.astype(jnp.bfloat16)
     rest = series - high.astype(jnp.float32)
     middle = rest.astype(jnp.bfloat16)
     low = (rest - middle.astype(jnp.float32)).astype(jnp.bfloat16)
-    sums = jnp.dot(
-        jnp.concatenate([high, middle, low], axis=0),
-        triangle_ref[...],
-        preferred_element_type=jnp.float32,
-    )
-    prefix = sums[:trials] + (sums[trials : 2 * trials] + sums[2 * trials :])
-    columns = [prefix[:, LANES * m : LANES * (m + 1)] for m in range(3)]
-    lane = lax.broadcasted_iota(jnp.int32, (trials, LANES), 1)
-    for index in range(out_ref.shape[0]):
-        turn = jnp.broadcast_to(turn_ref[index : index + 1, :], (trials, LANES))
-        scale = jnp.broadcast_to(scale_ref[index : index + 1, :], (trials, LANES))
-        turned = [jnp.take_along_axis(column, turn, axis=1) for column in columns]
-        inside = turn > lane
-        for m in range(2):
-            upper = jnp.where(inside, turned[m], turned[m + 1])
-            out_ref[index, :, LANES * m : LANES * (m + 1)] = (
-                (upper - columns[m]) * scale
-            ).astype(jnp.bfloat16)
+    terms = (high, middle, low)
+    reach = band_ref.shape[0]
+    halves = range(0, steps, LANES)
+    windows = jnp.concatenate([term[:, t : t + reach] for t in halves for term in terms], axis=0)
+    sums = jnp.dot(windows, band_ref[...], preferred_element_type=jnp.float32)
+    sums = sums.reshape(len(halves), len(terms), trials, count * LANES)
+    for index in range(count):
+        columns = slice(LANES * index, LANES * (index + 1))
+        scale = scale_ref[index : index + 1, :]
+        for half, t in enumerate(halves):
+            first, second, third = (sums[half, term, :, columns] for term in range(len(terms)))
+            out_ref[index, :, t : t + LANES] = ((first + (second + third)) * scale).astype(jnp.bfloat16)
 
 
 VMEM = pl.BlockSpec(memory_space=pltpu.VMEM)
@@ -185,7 +182,6 @@
     nblk = coarse_delay.shape[1]
     nsub, _, trials = fine_delay.shape
     count = widths.shape[0]
-    length = steps + WMAX
     by_block = coarse_delay.T
     fine = fine_delay.reshape(nsub, trials).T
     block = jax.ShapeDtypeStruct((nblk, steps), jnp.float32)
@@ -199,7 +195,7 @@
     sources = [pltpu.with_memory_space_constraint(x, pltpu.HBM) for x in (spectra, by_block)]
     own, sent = pl.pallas_call(
         sender_kernel,
-        out_shape=[block] * 2,
+        out_shape=[block, jax.ShapeDtypeStruct((nblk, steps), jnp.bfloat16)],
         in_specs=[HBM] * 2,
         out_specs=[VMEM] * 2,
         scratch_shapes=scratch,
@@ -219,16 +215,15 @@
         cost_estimate=pl.CostEstimate(flops=1 << 30, bytes_accessed=1 << 20, transcendentals=0),
         name="first_sums",
     )(*sources, own)
-    selector, triangle, turn, scale = pl.pallas_call(
+    selector, band, scale = pl.pallas_call(
         ready_kernel,
         out_shape=[
             jax.ShapeDtypeStruct((Q2 * trials, R2 * nsub), jnp.bfloat16),
-            jax.ShapeDtypeStruct((length, length), jnp.bfloat16),
-            jax.ShapeDtypeStruct((count, LANES), jnp.int32),
+            jax.ShapeDtypeStruct((LANES + WMAX, count * LANES), jnp.bfloat16),
             jax.ShapeDtypeStruct((count, LANES), jnp.float32),
         ],
         in_specs=[HBM] * 2,
-        out_specs=[VMEM] * 4,
+        out_specs=[VMEM] * 3,
         scratch_shapes=[
             pltpu.VMEM(fine.shape, fine.dtype),
             pltpu.SMEM(widths.shape, widths.dtype),
@@ -246,7 +241,7 @@
         scratch_shapes=[pltpu.VMEM((nblk * CHUNKS, LANES), jnp.float32)],
         compiler_params=PARAMS,
         name="join",
-    )(own, following, turn)
+    )(own, following, scale)
     groups = lax.axis_size("chan")
     received = lax.all_to_all(
         subbands,
@@ -259,12 +254,12 @@
     return pl.pallas_call(
         trial_kernel,
         out_shape=jax.ShapeDtypeStruct((count, trials, steps), jnp.bfloat16),
-        in_specs=[VMEM] * 5,
+        in_specs=[VMEM] * 4,
         out_specs=VMEM,
         scratch_shapes=[pltpu.VMEM((nsub * CHUNKS, LANES), jnp.float32)],
         compiler_params=PARAMS,
         name="trials",
-    )(received, selector, triangle, turn, scale)
+    )(received, selector, band, scale)
 
 
 def solution(mesh):

time: 27.3 us -> 26.7 us (0.978)
  waiting for transfers between devices: 4.36 us -> 3.77 us
    ppermute x1, waiting for transfers between devices: 4.36 us -> 3.77 us  [per_device(): lax.ppermute(sent, 'tm', [(z + 1, z) for z in range(blocks - 1)])]
  transfers between devices with their start and end apart: 1 -> 1, of which waited for: 1 -> 1; matrix products, arithmetic and copies ran while one was open for 0% -> 0% of each run, Pallas kernels for 11% -> 12%
where the time goes in v5:
time: 26.7 us; the launch traced here: 26.4 us
  blocking collectives  16.7 us (63%)
  Pallas kernels  4.61 us (17%)
  waiting for transfers between devices  3.77 us (14%)
  starting transfers between devices  1.29 us (5%)
    all_to_all x1, blocking collectives, per_device(): lax.all_to_all(subbands, 'chan', split_axis=0, concat_axis=0, tiled=True,...  16.7 us
    ppermute x1, waiting for transfers between devices, per_device(): lax.ppermute(sent, 'tm', [(z + 1, z) for z in range(blocks - 1)])  3.77 us
    pallas_call x1, Pallas kernels, per_device(): pl.pallas_call(first_kernel, out_shape=block, in_specs=[HBM] * 2 + [VMEM]...  2.06 us
    pallas_call x1, Pallas kernels, per_device(): pl.pallas_call(trial_kernel, out_shape=jax.ShapeDtypeStruct((count, trial...  1.32 us
    ppermute x1, starting transfers between devices, per_device(): lax.ppermute(sent, 'tm', [(z + 1, z) for z in range(blocks - 1)])  1.29 us
    pallas_call x1, Pallas kernels, per_device(): pl.pallas_call(ready_kernel, out_shape=[jax.ShapeDtypeStruct((Q2 * trials...  1.13 us
  transfers between devices with their start and end apart: 1, of which 1 were waited for; matrix products, arithmetic and copies ran while one was open for 0% of the time, Pallas kernels for 12%

profile of v5, /device:TPU:1, one launch (start us, length us, event | category | flops | bytes accessed | tf_op | source)
XLA Modules:
  0.0 26.4 jit_solution(3690722590876612061)
XLA Ops:
  0.0 1.3 %collective-permute-start = (bf16[64,256]{1,0:T(8,128)(2,1)S(1)}, bf16[64,256]{1,0:T(8,128)(2,1)S(1)}, u32[]{:S(2)}, u32[]{:S(2)}) collective-permute-start(bf16[64,256]{1,0:T(8,128)(2,1)S(1)} %get-tuple-element.11), channel_id=1, source_target_pairs={{1,0},{2,1},{3,2},{4,3},{5,4},{6,5},{7,6},{9,8},{10,9},{11,10},{12... | collective-permute-start | bytes 98312 | tf_op jit(solution)/shard_map/ppermute | solution.py:206
  1.3 2.1 %first_sums.1.own_ref = f32[64,256]{1,0:T(8,128)S(1)} custom-call(bf16[256,256]{1,0:T(8,128)(2,1)} %spectra_hbm.3, s32[64,256]{1,0:T(8,128)} %bitcast.9, f32[64,256]{1,0:T(8,128)S(1)} %get-tuple-element.10.sums_ref), custom_call_target="tpu_custom_call", output_to_operand_aliasing={{}: (2, {})} | custom-call | flops 1073741824 | bytes 1048576 | tf_op jit(solution)/shard_map/first_sums/pallas_call | solution.py:207
  3.4 1.1 %ready.1 = (bf16[256,256]{1,0:T(8,128)(2,1)S(1)}, bf16[256,1024]{1,0:T(8,128)(2,1)S(1)}, f32[8,128]{1,0:T(8,128)S(1)}) custom-call(s32[32,64]{1,0:T(8,128)} %bitcast.10, s32[8]{0:T(128)} %widths_hbm.1), custom_call_target="tpu_custom_call" | custom-call | flops 1073741824 | bytes 1048576 | tf_op jit(solution)/shard_map/ready/pallas_call | solution.py:218
  4.5 3.8 %collective-permute-done.next_ref = bf16[64,256]{1,0:T(8,128)(2,1)S(1)} collective-permute-done((bf16[64,256]{1,0:T(8,128)(2,1)S(1)}, bf16[64,256]{1,0:T(8,128)(2,1)S(1)}, u32[]{:S(2)}, u32[]{:S(2)}) %collective-permute-start) | collective-permute-done | bytes 32800 | tf_op jit(solution)/shard_map/ppermute | solution.py:206
  8.3 0.1 join.1
  8.4 16.7 %all_to_all.11 = bf16[64,4,128]{2,1,0:T(4,128)(2,1)S(1)} all-to-all(bf16[64,4,128]{2,1,0:T(4,128)(2,1)S(1)} %bitcast.6), channel_id=1, replica_groups={{328,336,344,352,360,368,376,384,392,400,408,416,424,432,440,448,456,46..., dimensions={0} | all-to-all | bytes 131072 | tf_op jit(solution)/shard_map/all_to_all | solution.py:246
  25.1 1.3 %trials.1 = bf16[8,32,256]{2,1,0:T(8,128)(2,1)} custom-call(bf16[256,128]{1,0:T(8,128)(2,1)S(1)} %bitcast.7, bf16[256,256]{1,0:T(8,128)(2,1)S(1)} %get-tuple-element.13.selector_ref, bf16[256,1024]{1,0:T(8,128)(2,1)S(1)} %get-tuple-element.14.band_ref, f32[8,128]{1,0:T(8,128)S(1)} %get-tuple-element.12.ready_ref.scale_ref), custom_call_target="tpu_custom_call" | custom-call | tf_op jit(solution)/shard_map/trials/pallas_call | solution.py:254
  (1 shorter events, 0.0 us)
Async XLA Ops:
  0.0 8.3 %collective-permute-start = (bf16[64,256]{1,0:T(8,128)(2,1)S(1)}, bf16[64,256]{1,0:T(8,128)(2,1)S(1)}, u32[]{:S(2)}, u32[]{:S(2)}) collective-permute-start(bf16[64,256]{1,0:T(8,128)(2,1)S(1)} %get-tuple-element.11), channel_id=1, source_target_pairs={{1,0},{2,1},{3,2},{4,3},{5,4},{6,5},{7,6},{9,8},{10,9},{11,10},{12... | collective-permute-start | bytes 98312 | tf_op jit(solution)/shard_map/ppermute | solution.py:206

commit v6 on v5

--- a/solution.py
+++ b/solution.py
@@ -18,7 +18,7 @@
 Q1 = (D1MAX + 1) // R1
 R2 = 4
 Q2 = (D2MAX + 1) // R2
-ROOT = 41
+BASE = 42
 CHUNKS = 4
 
 
@@ -34,9 +34,15 @@
     return jnp.concatenate([x[:, by:], x[:, :by]], axis=1)
 
 
-def from_root(x, axis):
-    first, second = jnp.split(x, [ROOT], axis=axis)
-    return jnp.concatenate([second, first], axis=axis)
+def listed(i, count):
+    return (i + BASE) % count ^ 1
+
+
+def in_listed_order(x):
+    count = x.shape[0]
+    x = jnp.concatenate([x[BASE:], x[:BASE]], axis=0)
+    even = lax.broadcasted_iota(jnp.int32, x.shape, 0) % 2 == 0
+    return jnp.where(even, pltpu.roll(x, count - 1, 0), pltpu.roll(x, 1, 0))
 
 
 def one_hot(delay, level):
@@ -58,7 +64,7 @@
     nblk, steps = out_ref.shape
     last = steps - LANES
     spectra = spectra_ref[...]
-    delay = from_root(delay_ref[...], 0).astype(jnp.bfloat16)
+    delay = in_listed_order(delay_ref[...]).astype(jnp.bfloat16)
     lane = lax.broadcasted_iota(jnp.int32, (1, LANES), 1)
     for r in range(R1):
         selector = jnp.concatenate([one_hot(delay, float(R1 * q + r)) for q in range(Q1)], axis=0)
@@ -82,7 +88,10 @@
         )
     out_ref[...] = total[:, LANES:]
     if sent_ref is not None:
-        sent_ref[...] = total[:, LANES - MARGIN : LANES - MARGIN + steps].astype(jnp.bfloat16)
+        around = jnp.where(lane < LANES - MARGIN, total[:, 2 * LANES :], total[:, :LANES])
+        sent_ref[...] = jnp.concatenate([total[:, LANES : 2 * LANES], around], axis=1).astype(
+            jnp.bfloat16
+        )
 
 
 def sender_kernel(spectra_hbm, delay_hbm, out_ref, sent_ref, *scratch):
@@ -108,7 +117,12 @@
         copy.start()
     for copy in copies:
         copy.wait()
-    fine = from_root(fine_ref[...], 1)
+    nsub = fine_ref.shape[1]
+    subband = lax.broadcasted_iota(jnp.int32, (nsub, nsub), 0)
+    place = lax.broadcasted_iota(jnp.int32, (nsub, nsub), 1)
+    place = 2 * (place % (nsub // 2)) + place // (nsub // 2)
+    order = jnp.where(subband == listed(place, nsub), 1.0, 0.0).astype(jnp.bfloat16)
+    fine = jnp.dot(fine_ref[...].astype(jnp.bfloat16), order, preferred_element_type=jnp.float32)
     fine = jnp.concatenate([fine - r for r in range(R2)], axis=1).astype(jnp.bfloat16)
     selector_ref[...] = jnp.concatenate([one_hot(fine, float(R2 * q)) for q in range(Q2)], axis=0)
     shape = (band_ref.shape[0], LANES)
@@ -124,20 +138,11 @@
 
 def join_kernel(own_ref, next_ref, ready_ref, out_ref, rows_ref):
     del ready_ref
-    nblk, steps = own_ref.shape
-    left = steps - MARGIN - LANES
-    total = jnp.concatenate(
-        [
-            jnp.zeros((nblk, left), jnp.float32),
-            next_ref[...].astype(jnp.float32),
-            jnp.zeros((nblk, 3 * LANES - left - steps), jnp.float32),
-        ],
-        axis=1,
-    )
-    rows_ref[pl.ds(0, nblk, stride=CHUNKS), :] = own_ref[:, :LANES]
-    rows_ref[pl.ds(1, nblk, stride=CHUNKS), :] = own_ref[:, LANES:] + total[:, :LANES]
-    rows_ref[pl.ds(2, nblk, stride=CHUNKS), :] = total[:, LANES : 2 * LANES]
-    rows_ref[pl.ds(3, nblk, stride=CHUNKS), :] = total[:, 2 * LANES :]
+    nblk = own_ref.shape[0]
+    following = next_ref[...].astype(jnp.float32)
+    chunks = [own_ref[:, :LANES], own_ref[:, LANES:], following[:, :LANES], following[:, LANES:]]
+    for m, chunk in enumerate(chunks):
+        rows_ref[pl.ds(m, nblk, stride=CHUNKS), :] = chunk
     out_ref[...] = rows_ref[...].astype(jnp.bfloat16)
 
 
@@ -145,8 +150,23 @@
     count, trials, steps = out_ref.shape
     nsub = sub_ref.shape[0] // CHUNKS
     rows_ref[...] = sub_ref[...].astype(jnp.float32)
+
+    def chunk(m, first, second):
+        return jnp.concatenate(
+            [rows_ref[pl.ds(CHUNKS * odd + m, nsub // 2, stride=2 * CHUNKS), :] for odd in (first, second)],
+            axis=0,
+        )
+
+    around = chunk(3, 1, 0)
+    lane = lax.broadcasted_iota(jnp.int32, around.shape, 1)
     sub = jnp.concatenate(
-        [rows_ref[pl.ds(m, nsub, stride=CHUNKS), :] for m in range(CHUNKS)], axis=1
+        [
+            chunk(0, 0, 1),
+            chunk(1, 0, 1) + jnp.where(lane < LANES - MARGIN, 0.0, around),
+            chunk(2, 1, 0),
+            around,
+        ],
+        axis=1,
     ).astype(jnp.bfloat16)
     shifted = jnp.concatenate([shift_left(sub, r) for r in range(R2)], axis=0)
     parts = jnp.dot(selector_ref[...], shifted, preferred_element_type=jnp.float32)
@@ -203,7 +223,16 @@
         name="sender_sums",
     )(*sources)
     blocks = lax.axis_size("tm")
-    following = lax.ppermute(sent, "tm", [(z + 1, z) for z in range(blocks - 1)])
+    groups = lax.axis_size("chan")
+    following = lax.ppermute(
+        sent,
+        ("chan", "tm"),
+        [
+            (c * blocks + z + 1, (c ^ 1) * blocks + z)
+            for c in range(groups)
+            for z in range(blocks - 1)
+        ],
+    )
     own = pl.pallas_call(
         first_kernel,
         out_shape=block,
@@ -242,14 +271,13 @@
         compiler_params=PARAMS,
         name="join",
     )(own, following, scale)
-    groups = lax.axis_size("chan")
     received = lax.all_to_all(
         subbands,
         "chan",
         split_axis=0,
         concat_axis=0,
         tiled=True,
-        axis_index_groups=[[(i + ROOT) % groups for i in range(groups)]],
+        axis_index_groups=[[listed(i, groups) for i in range(groups)]],
     )
     return pl.pallas_call(
         trial_kernel,

time: 26.7 us -> 25.9 us (0.970)
  blocking collectives: 16.7 us -> 15.2 us
  waiting for transfers between devices: 3.77 us -> 4.5 us
    all_to_all x1, blocking collectives: 16.7 us -> 15.2 us  [per_device(): lax.all_to_all(subbands, 'chan', split_axis=0, concat_axis=0, tiled=True,...]
    ppermute x1, waiting for transfers between devices: 3.77 us -> 4.5 us  [per_device(): lax.ppermute(sent, ('chan', 'tm'), [(c * blocks + z + 1, (c ^ 1) * blocks...]
  transfers between devices with their start and end apart: 1 -> 1, of which waited for: 1 -> 1; matrix products, arithmetic and copies ran while one was open for 0% -> 0% of each run, Pallas kernels for 12% -> 13%
where the time goes in v6:
time: 25.9 us; the launch traced here: 25.6 us
  blocking collectives  15.2 us (59%)
  Pallas kernels  4.61 us (18%)
  waiting for transfers between devices  4.5 us (17%)
  starting transfers between devices  1.29 us (5%)
    all_to_all x1, blocking collectives, per_device(): lax.all_to_all(subbands, 'chan', split_axis=0, concat_axis=0, tiled=True,...  15.2 us
    ppermute x1, waiting for transfers between devices, per_device(): lax.ppermute(sent, ('chan', 'tm'), [(c * blocks + z + 1, (c ^ 1) * blocks...  4.5 us
    pallas_call x1, Pallas kernels, per_device(): pl.pallas_call(first_kernel, out_shape=block, in_specs=[HBM] * 2 + [VMEM]...  2.06 us
    pallas_call x1, Pallas kernels, per_device(): pl.pallas_call(trial_kernel, out_shape=jax.ShapeDtypeStruct((count, trial...  1.33 us
    ppermute x1, starting transfers between devices, per_device(): lax.ppermute(sent, ('chan', 'tm'), [(c * blocks + z + 1, (c ^ 1) * blocks...  1.29 us
    pallas_call x1, Pallas kernels, per_device(): pl.pallas_call(ready_kernel, out_shape=[jax.ShapeDtypeStruct((Q2 * trials...  1.18 us
  transfers between devices with their start and end apart: 1, of which 1 were waited for; matrix products, arithmetic and copies ran while one was open for 0% of the time, Pallas kernels for 13%

profile of v6, /device:TPU:1, one launch (start us, length us, event | category | flops | bytes accessed | tf_op | source)
XLA Modules:
  0.0 25.6 jit_solution(17859019817936889211)
XLA Ops:
  0.0 1.3 %collective-permute-start = (bf16[64,256]{1,0:T(8,128)(2,1)S(1)}, bf16[64,256]{1,0:T(8,128)(2,1)S(1)}, u32[]{:S(2)}, u32[]{:S(2)}) collective-permute-start(bf16[64,256]{1,0:T(8,128)(2,1)S(1)} %get-tuple-element.11), channel_id=1, source_target_pairs={{1,8},{2,9},{3,10},{4,11},{5,12},{6,13},{7,14},{9,0},{10,1},{11,2}... | collective-permute-start | bytes 98312 | tf_op jit(solution)/shard_map/ppermute | solution.py:227
  1.3 2.1 %first_sums.1.own_ref = f32[64,256]{1,0:T(8,128)S(1)} custom-call(bf16[256,256]{1,0:T(8,128)(2,1)} %spectra_hbm.3, s32[64,256]{1,0:T(8,128)} %bitcast.9, f32[64,256]{1,0:T(8,128)S(1)} %get-tuple-element.10.sums_ref), custom_call_target="tpu_custom_call", output_to_operand_aliasing={{}: (2, {})} | custom-call | flops 1073741824 | bytes 1048576 | tf_op jit(solution)/shard_map/first_sums/pallas_call | solution.py:236
  3.4 1.2 %ready.1 = (bf16[256,256]{1,0:T(8,128)(2,1)S(1)}, bf16[256,1024]{1,0:T(8,128)(2,1)S(1)}, f32[8,128]{1,0:T(8,128)S(1)}) custom-call(s32[32,64]{1,0:T(8,128)} %bitcast.10, s32[8]{0:T(128)} %widths_hbm.1), custom_call_target="tpu_custom_call" | custom-call | flops 1073741824 | bytes 1048576 | tf_op jit(solution)/shard_map/ready/pallas_call | solution.py:247
  4.6 4.5 %collective-permute-done.next_ref = bf16[64,256]{1,0:T(8,128)(2,1)S(1)} collective-permute-done((bf16[64,256]{1,0:T(8,128)(2,1)S(1)}, bf16[64,256]{1,0:T(8,128)(2,1)S(1)}, u32[]{:S(2)}, u32[]{:S(2)}) %collective-permute-start) | collective-permute-done | bytes 32800 | tf_op jit(solution)/shard_map/ppermute | solution.py:227
  9.1 15.2 %all_to_all.11 = bf16[64,4,128]{2,1,0:T(4,128)(2,1)S(1)} all-to-all(bf16[64,4,128]{2,1,0:T(4,128)(2,1)S(1)} %bitcast.6), channel_id=1, replica_groups={{344,336,360,352,376,368,392,384,408,400,424,416,440,432,456,448,472,46..., dimensions={0} | all-to-all | bytes 131072 | tf_op jit(solution)/shard_map/all_to_all | solution.py:274
  24.3 1.3 %trials.1 = bf16[8,32,256]{2,1,0:T(8,128)(2,1)} custom-call(bf16[256,128]{1,0:T(8,128)(2,1)S(1)} %bitcast.7, bf16[256,256]{1,0:T(8,128)(2,1)S(1)} %get-tuple-element.13.selector_ref, bf16[256,1024]{1,0:T(8,128)(2,1)S(1)} %get-tuple-element.14.band_ref, f32[8,128]{1,0:T(8,128)S(1)} %get-tuple-element.12.ready_ref.scale_ref), custom_call_target="tpu_custom_call" | custom-call | tf_op jit(solution)/shard_map/trials/pallas_call | solution.py:282
  (2 shorter events, 0.0 us)
Async XLA Ops:
  0.0 9.1 %collective-permute-start = (bf16[64,256]{1,0:T(8,128)(2,1)S(1)}, bf16[64,256]{1,0:T(8,128)(2,1)S(1)}, u32[]{:S(2)}, u32[]{:S(2)}) collective-permute-start(bf16[64,256]{1,0:T(8,128)(2,1)S(1)} %get-tuple-element.11), channel_id=1, source_target_pairs={{1,8},{2,9},{3,10},{4,11},{5,12},{6,13},{7,14},{9,0},{10,1},{11,2}... | collective-permute-start | bytes 98312 | tf_op jit(solution)/shard_map/ppermute | solution.py:227

commit v7 on v6

--- a/solution.py
+++ b/solution.py
@@ -53,10 +53,14 @@
     spectra_hbm, delay_hbm, out_ref, sent_ref,
     spectra_ref, delay_ref, acc_ref, before_ref, sems,
 ):
-    copies = [
-        pltpu.make_async_copy(spectra_hbm, spectra_ref, sems.at[0]),
-        pltpu.make_async_copy(delay_hbm, delay_ref, sems.at[1]),
-    ]
+    copies = []
+    for source, target, cuts in ((delay_hbm, delay_ref, 2), (spectra_hbm, spectra_ref, 4)):
+        rows = source.shape[0] // cuts
+        for cut in range(cuts):
+            part = pl.ds(rows * cut, rows)
+            copies.append(
+                pltpu.make_async_copy(source.at[part], target.at[part], sems.at[len(copies)])
+            )
     for copy in copies:
         copy.start()
     for copy in copies:
@@ -131,7 +135,7 @@
         width = widths_ref[index]
         counts = jnp.logical_and(ahead >= 0, ahead < width)
         band_ref[:, LANES * index : LANES * (index + 1)] = jnp.where(counts, 1.0, 0.0).astype(jnp.bfloat16)
-        scale_ref[index : index + 1, :] = 1.0 / jnp.sqrt(
+        scale_ref[index : index + 1, :] = (1.0 / math.sqrt(CHANNELS)) / jnp.sqrt(
             jnp.full((1, LANES), width).astype(jnp.float32)
         )
 
@@ -167,13 +171,15 @@
             around,
         ],
         axis=1,
-    ).astype(jnp.bfloat16)
-    shifted = jnp.concatenate([shift_left(sub, r) for r in range(R2)], axis=0)
+    )
+    shifted = jnp.concatenate(
+        [turn_left(sub, r).astype(jnp.bfloat16) for r in range(R2)], axis=0
+    )
     parts = jnp.dot(selector_ref[...], shifted, preferred_element_type=jnp.float32)
     series = parts[:trials]
     for q in range(1, Q2):
         series = series + shift_left(parts[trials * q : trials * (q + 1)], R2 * q)
-    series = series[:, : steps + WMAX] * (1.0 / math.sqrt(CHANNELS))
+    series = series[:, : steps + WMAX]
     high = series.astype(jnp.bfloat16)
     rest = series - high.astype(jnp.float32)
     middle = rest.astype(jnp.bfloat16)
@@ -210,7 +216,7 @@
         pltpu.VMEM(by_block.shape, by_block.dtype),
         pltpu.VMEM((Q1 * nblk, steps), jnp.float32),
         pltpu.VMEM((Q1 * nblk, LANES), jnp.float32),
-        pltpu.SemaphoreType.DMA((2,)),
+        pltpu.SemaphoreType.DMA((6,)),
     ]
     sources = [pltpu.with_memory_space_constraint(x, pltpu.HBM) for x in (spectra, by_block)]
     own, sent = pl.pallas_call(

time: 25.9 us -> 25.9 us (level)
  no operation moved by 1% of the time
where the time goes in v7:
time: 25.9 us; the launch traced here: 25.7 us
  blocking collectives  15.3 us (59%)
  Pallas kernels  4.61 us (18%)
  waiting for transfers between devices  4.46 us (17%)
  starting transfers between devices  1.29 us (5%)
    all_to_all x1, blocking collectives, per_device(): lax.all_to_all(subbands, 'chan', split_axis=0, concat_axis=0, tiled=True,...  15.3 us
    ppermute x1, waiting for transfers between devices, per_device(): lax.ppermute(sent, ('chan', 'tm'), [(c * blocks + z + 1, (c ^ 1) * blocks...  4.46 us
    pallas_call x1, Pallas kernels, per_device(): pl.pallas_call(first_kernel, out_shape=block, in_specs=[HBM] * 2 + [VMEM]...  2.03 us
    pallas_call x1, Pallas kernels, per_device(): pl.pallas_call(trial_kernel, out_shape=jax.ShapeDtypeStruct((count, trial...  1.32 us
    ppermute x1, starting transfers between devices, per_device(): lax.ppermute(sent, ('chan', 'tm'), [(c * blocks + z + 1, (c ^ 1) * blocks...  1.29 us
    pallas_call x1, Pallas kernels, per_device(): pl.pallas_call(ready_kernel, out_shape=[jax.ShapeDtypeStruct((Q2 * trials...  1.19 us
  transfers between devices with their start and end apart: 1, of which 1 were waited for; matrix products, arithmetic and copies ran while one was open for 0% of the time, Pallas kernels for 13%

profile of v7, /device:TPU:1, one launch (start us, length us, event | category | flops | bytes accessed | tf_op | source)
XLA Modules:
  0.0 25.7 jit_solution(4582567585548391043)
XLA Ops:
  0.0 0.1 sender_sums.1
  0.1 1.3 %collective-permute-start = (bf16[64,256]{1,0:T(8,128)(2,1)S(1)}, bf16[64,256]{1,0:T(8,128)(2,1)S(1)}, u32[]{:S(2)}, u32[]{:S(2)}) collective-permute-start(bf16[64,256]{1,0:T(8,128)(2,1)S(1)} %get-tuple-element.11), channel_id=1, source_target_pairs={{1,8},{2,9},{3,10},{4,11},{5,12},{6,13},{7,14},{9,0},{10,1},{11,2}... | collective-permute-start | bytes 98312 | tf_op jit(solution)/shard_map/ppermute | solution.py:233
  1.4 2.0 %first_sums.1.own_ref = f32[64,256]{1,0:T(8,128)S(1)} custom-call(bf16[256,256]{1,0:T(8,128)(2,1)} %spectra_hbm.3, s32[64,256]{1,0:T(8,128)} %bitcast.9, f32[64,256]{1,0:T(8,128)S(1)} %get-tuple-element.10.sums_ref), custom_call_target="tpu_custom_call", output_to_operand_aliasing={{}: (2, {})} | custom-call | flops 1073741824 | bytes 1048576 | tf_op jit(solution)/shard_map/first_sums/pallas_call | solution.py:242
  3.4 1.2 %ready.1 = (bf16[256,256]{1,0:T(8,128)(2,1)S(1)}, bf16[256,1024]{1,0:T(8,128)(2,1)S(1)}, f32[8,128]{1,0:T(8,128)S(1)}) custom-call(s32[32,64]{1,0:T(8,128)} %bitcast.10, s32[8]{0:T(128)} %widths_hbm.1), custom_call_target="tpu_custom_call" | custom-call | flops 1073741824 | bytes 1048576 | tf_op jit(solution)/shard_map/ready/pallas_call | solution.py:253
  4.6 4.5 %collective-permute-done.next_ref = bf16[64,256]{1,0:T(8,128)(2,1)S(1)} collective-permute-done((bf16[64,256]{1,0:T(8,128)(2,1)S(1)}, bf16[64,256]{1,0:T(8,128)(2,1)S(1)}, u32[]{:S(2)}, u32[]{:S(2)}) %collective-permute-start) | collective-permute-done | bytes 32800 | tf_op jit(solution)/shard_map/ppermute | solution.py:233
  9.1 15.3 %all_to_all.11 = bf16[64,4,128]{2,1,0:T(4,128)(2,1)S(1)} all-to-all(bf16[64,4,128]{2,1,0:T(4,128)(2,1)S(1)} %bitcast.6), channel_id=1, replica_groups={{344,336,360,352,376,368,392,384,408,400,424,416,440,432,456,448,472,46..., dimensions={0} | all-to-all | bytes 131072 | tf_op jit(solution)/shard_map/all_to_all | solution.py:280
  24.3 1.3 %trials.1 = bf16[8,32,256]{2,1,0:T(8,128)(2,1)} custom-call(bf16[256,128]{1,0:T(8,128)(2,1)S(1)} %bitcast.7, bf16[256,256]{1,0:T(8,128)(2,1)S(1)} %get-tuple-element.13.selector_ref, bf16[256,1024]{1,0:T(8,128)(2,1)S(1)} %get-tuple-element.14.band_ref, f32[8,128]{1,0:T(8,128)S(1)} %get-tuple-element.12.ready_ref.scale_ref), custom_call_target="tpu_custom_call" | custom-call | tf_op jit(solution)/shard_map/trials/pallas_call | solution.py:288
  (1 shorter events, 0.0 us)
Async XLA Ops:
  0.1 9.0 %collective-permute-start = (bf16[64,256]{1,0:T(8,128)(2,1)S(1)}, bf16[64,256]{1,0:T(8,128)(2,1)S(1)}, u32[]{:S(2)}, u32[]{:S(2)}) collective-permute-start(bf16[64,256]{1,0:T(8,128)(2,1)S(1)} %get-tuple-element.11), channel_id=1, source_target_pairs={{1,8},{2,9},{3,10},{4,11},{5,12},{6,13},{7,14},{9,0},{10,1},{11,2}... | collective-permute-start | bytes 98312 | tf_op jit(solution)/shard_map/ppermute | solution.py:233

commit v8 on v6

--- a/solution.py
+++ b/solution.py
@@ -131,7 +131,7 @@
         width = widths_ref[index]
         counts = jnp.logical_and(ahead >= 0, ahead < width)
         band_ref[:, LANES * index : LANES * (index + 1)] = jnp.where(counts, 1.0, 0.0).astype(jnp.bfloat16)
-        scale_ref[index : index + 1, :] = 1.0 / jnp.sqrt(
+        scale_ref[index : index + 1, :] = (1.0 / math.sqrt(CHANNELS)) / jnp.sqrt(
             jnp.full((1, LANES), width).astype(jnp.float32)
         )
 
@@ -167,18 +167,17 @@
             around,
         ],
         axis=1,
-    ).astype(jnp.bfloat16)
-    shifted = jnp.concatenate([shift_left(sub, r) for r in range(R2)], axis=0)
+    )
+    shifted = jnp.concatenate(
+        [turn_left(sub, r).astype(jnp.bfloat16) for r in range(R2)], axis=0
+    )
     parts = jnp.dot(selector_ref[...], shifted, preferred_element_type=jnp.float32)
     series = parts[:trials]
     for q in range(1, Q2):
         series = series + shift_left(parts[trials * q : trials * (q + 1)], R2 * q)
-    series = series[:, : steps + WMAX] * (1.0 / math.sqrt(CHANNELS))
+    series = series[:, : steps + WMAX]
     high = series.astype(jnp.bfloat16)
-    rest = series - high.astype(jnp.float32)
-    middle = rest.astype(jnp.bfloat16)
-    low = (rest - middle.astype(jnp.float32)).astype(jnp.bfloat16)
-    terms = (high, middle, low)
+    terms = (high, (series - high.astype(jnp.float32)).astype(jnp.bfloat16))
     reach = band_ref.shape[0]
     halves = range(0, steps, LANES)
     windows = jnp.concatenate([term[:, t : t + reach] for t in halves for term in terms], axis=0)
@@ -188,8 +187,8 @@
         columns = slice(LANES * index, LANES * (index + 1))
         scale = scale_ref[index : index + 1, :]
         for half, t in enumerate(halves):
-            first, second, third = (sums[half, term, :, columns] for term in range(len(terms)))
-            out_ref[index, :, t : t + LANES] = ((first + (second + third)) * scale).astype(jnp.bfloat16)
+            first, second = (sums[half, term, :, columns] for term in range(len(terms)))
+            out_ref[index, :, t : t + LANES] = ((first + second) * scale).astype(jnp.bfloat16)
 
 
 VMEM = pl.BlockSpec(memory_space=pltpu.VMEM)

time: 25.9 us -> 25.8 us (level)
  no operation moved by 1% of the time
where the time goes in v8:
time: 25.8 us; the launch traced here: 25.6 us
  blocking collectives  15.2 us (59%)
  Pallas kernels  4.58 us (18%)
  waiting for transfers between devices  4.5 us (17%)
  starting transfers between devices  1.29 us (5%)
    all_to_all x1, blocking collectives, per_device(): lax.all_to_all(subbands, 'chan', split_axis=0, concat_axis=0, tiled=True,...  15.2 us
    ppermute x1, waiting for transfers between devices, per_device(): lax.ppermute(sent, ('chan', 'tm'), [(c * blocks + z + 1, (c ^ 1) * blocks...  4.5 us
    pallas_call x1, Pallas kernels, per_device(): pl.pallas_call(first_kernel, out_shape=block, in_specs=[HBM] * 2 + [VMEM]...  2.06 us
    pallas_call x1, Pallas kernels, per_device(): pl.pallas_call(trial_kernel, out_shape=jax.ShapeDtypeStruct((count, trial...  1.3 us
    ppermute x1, starting transfers between devices, per_device(): lax.ppermute(sent, ('chan', 'tm'), [(c * blocks + z + 1, (c ^ 1) * blocks...  1.29 us
    pallas_call x1, Pallas kernels, per_device(): pl.pallas_call(ready_kernel, out_shape=[jax.ShapeDtypeStruct((Q2 * trials...  1.19 us
  transfers between devices with their start and end apart: 1, of which 1 were waited for; matrix products, arithmetic and copies ran while one was open for 0% of the time, Pallas kernels for 13%

profile of v8, /device:TPU:1, one launch (start us, length us, event | category | flops | bytes accessed | tf_op | source)
XLA Modules:
  0.0 25.6 jit_solution(12776954608232284107)
XLA Ops:
  0.0 1.3 %collective-permute-start = (bf16[64,256]{1,0:T(8,128)(2,1)S(1)}, bf16[64,256]{1,0:T(8,128)(2,1)S(1)}, u32[]{:S(2)}, u32[]{:S(2)}) collective-permute-start(bf16[64,256]{1,0:T(8,128)(2,1)S(1)} %get-tuple-element.11), channel_id=1, source_target_pairs={{1,8},{2,9},{3,10},{4,11},{5,12},{6,13},{7,14},{9,0},{10,1},{11,2}... | collective-permute-start | bytes 98312 | tf_op jit(solution)/shard_map/ppermute | solution.py:226
  1.3 2.1 %first_sums.1.own_ref = f32[64,256]{1,0:T(8,128)S(1)} custom-call(bf16[256,256]{1,0:T(8,128)(2,1)} %spectra_hbm.3, s32[64,256]{1,0:T(8,128)} %bitcast.9, f32[64,256]{1,0:T(8,128)S(1)} %get-tuple-element.10.sums_ref), custom_call_target="tpu_custom_call", output_to_operand_aliasing={{}: (2, {})} | custom-call | flops 1073741824 | bytes 1048576 | tf_op jit(solution)/shard_map/first_sums/pallas_call | solution.py:235
  3.4 1.2 %ready.1 = (bf16[256,256]{1,0:T(8,128)(2,1)S(1)}, bf16[256,1024]{1,0:T(8,128)(2,1)S(1)}, f32[8,128]{1,0:T(8,128)S(1)}) custom-call(s32[32,64]{1,0:T(8,128)} %bitcast.10, s32[8]{0:T(128)} %widths_hbm.1), custom_call_target="tpu_custom_call" | custom-call | flops 1073741824 | bytes 1048576 | tf_op jit(solution)/shard_map/ready/pallas_call | solution.py:246
  4.6 4.5 %collective-permute-done.next_ref = bf16[64,256]{1,0:T(8,128)(2,1)S(1)} collective-permute-done((bf16[64,256]{1,0:T(8,128)(2,1)S(1)}, bf16[64,256]{1,0:T(8,128)(2,1)S(1)}, u32[]{:S(2)}, u32[]{:S(2)}) %collective-permute-start) | collective-permute-done | bytes 32800 | tf_op jit(solution)/shard_map/ppermute | solution.py:226
  9.1 15.2 %all_to_all.11 = bf16[64,4,128]{2,1,0:T(4,128)(2,1)S(1)} all-to-all(bf16[64,4,128]{2,1,0:T(4,128)(2,1)S(1)} %bitcast.6), channel_id=1, replica_groups={{344,336,360,352,376,368,392,384,408,400,424,416,440,432,456,448,472,46..., dimensions={0} | all-to-all | bytes 131072 | tf_op jit(solution)/shard_map/all_to_all | solution.py:273
  24.3 1.3 %trials.1 = bf16[8,32,256]{2,1,0:T(8,128)(2,1)} custom-call(bf16[256,128]{1,0:T(8,128)(2,1)S(1)} %bitcast.7, bf16[256,256]{1,0:T(8,128)(2,1)S(1)} %get-tuple-element.13.selector_ref, bf16[256,1024]{1,0:T(8,128)(2,1)S(1)} %get-tuple-element.14.band_ref, f32[8,128]{1,0:T(8,128)S(1)} %get-tuple-element.12.ready_ref.scale_ref), custom_call_target="tpu_custom_call" | custom-call | tf_op jit(solution)/shard_map/trials/pallas_call | solution.py:281
  (2 shorter events, 0.0 us)
Async XLA Ops:
  0.0 9.1 %collective-permute-start = (bf16[64,256]{1,0:T(8,128)(2,1)S(1)}, bf16[64,256]{1,0:T(8,128)(2,1)S(1)}, u32[]{:S(2)}, u32[]{:S(2)}) collective-permute-start(bf16[64,256]{1,0:T(8,128)(2,1)S(1)} %get-tuple-element.11), channel_id=1, source_target_pairs={{1,8},{2,9},{3,10},{4,11},{5,12},{6,13},{7,14},{9,0},{10,1},{11,2}... | collective-permute-start | bytes 98312 | tf_op jit(solution)/shard_map/ppermute | solution.py:226

commit v9 on v8

--- a/solution.py
+++ b/solution.py
@@ -100,21 +100,23 @@
         own_sums(spectra_hbm, delay_hbm, out_ref, sent_ref, *scratch)
 
 
-def first_kernel(spectra_hbm, delay_hbm, sums_ref, out_ref, *scratch):
+def beside_kernel(
+    spectra_hbm, delay_hbm, sums_ref, fine_hbm, widths_hbm,
+    out_ref, selector_ref, band_ref, scale_ref,
+    fine_ref, widths_ref, load_sems, *scratch,
+):
     del sums_ref
+    copies = [
+        pltpu.make_async_copy(fine_hbm, fine_ref, load_sems.at[0]),
+        pltpu.make_async_copy(widths_hbm, widths_ref, load_sems.at[1]),
+    ]
+    for copy in copies:
+        copy.start()
 
     @pl.when(lax.axis_index("tm") == 0)
     def _():
         own_sums(spectra_hbm, delay_hbm, out_ref, None, *scratch)
 
-
-def ready_kernel(fine_hbm, widths_hbm, selector_ref, band_ref, scale_ref, fine_ref, widths_ref, sems):
-    copies = [
-        pltpu.make_async_copy(fine_hbm, fine_ref, sems.at[0]),
-        pltpu.make_async_copy(widths_hbm, widths_ref, sems.at[1]),
-    ]
-    for copy in copies:
-        copy.start()
     for copy in copies:
         copy.wait()
     nsub = fine_ref.shape[1]
@@ -136,8 +138,7 @@
         )
 
 
-def join_kernel(own_ref, next_ref, ready_ref, out_ref, rows_ref):
-    del ready_ref
+def join_kernel(own_ref, next_ref, out_ref, rows_ref):
     nblk = own_ref.shape[0]
     following = next_ref[...].astype(jnp.float32)
     chunks = [own_ref[:, :LANES], own_ref[:, LANES:], following[:, :LANES], following[:, LANES:]]
@@ -232,44 +233,36 @@
             for z in range(blocks - 1)
         ],
     )
-    own = pl.pallas_call(
-        first_kernel,
-        out_shape=block,
-        in_specs=[HBM] * 2 + [VMEM],
-        out_specs=VMEM,
-        scratch_shapes=scratch,
-        input_output_aliases={2: 0},
-        compiler_params=PARAMS,
-        cost_estimate=pl.CostEstimate(flops=1 << 30, bytes_accessed=1 << 20, transcendentals=0),
-        name="first_sums",
-    )(*sources, own)
-    selector, band, scale = pl.pallas_call(
-        ready_kernel,
+    own, selector, band, scale = pl.pallas_call(
+        beside_kernel,
         out_shape=[
+            block,
             jax.ShapeDtypeStruct((Q2 * trials, R2 * nsub), jnp.bfloat16),
             jax.ShapeDtypeStruct((LANES + WMAX, count * LANES), jnp.bfloat16),
             jax.ShapeDtypeStruct((count, LANES), jnp.float32),
         ],
-        in_specs=[HBM] * 2,
-        out_specs=[VMEM] * 3,
+        in_specs=[HBM] * 2 + [VMEM] + [HBM] * 2,
+        out_specs=[VMEM] * 4,
         scratch_shapes=[
             pltpu.VMEM(fine.shape, fine.dtype),
             pltpu.SMEM(widths.shape, widths.dtype),
             pltpu.SemaphoreType.DMA((2,)),
-        ],
+            *scratch,
+        ],
+        input_output_aliases={2: 0},
         compiler_params=PARAMS,
         cost_estimate=pl.CostEstimate(flops=1 << 30, bytes_accessed=1 << 20, transcendentals=0),
-        name="ready",
-    )(*(pltpu.with_memory_space_constraint(x, pltpu.HBM) for x in (fine, widths)))
+        name="beside",
+    )(*sources, own, *(pltpu.with_memory_space_constraint(x, pltpu.HBM) for x in (fine, widths)))
     subbands = pl.pallas_call(
         join_kernel,
         out_shape=jax.ShapeDtypeStruct((nblk * CHUNKS, LANES), jnp.bfloat16),
-        in_specs=[VMEM] * 3,
+        in_specs=[VMEM] * 2,
         out_specs=VMEM,
         scratch_shapes=[pltpu.VMEM((nblk * CHUNKS, LANES), jnp.float32)],
         compiler_params=PARAMS,
         name="join",
-    )(own, following, scale)
+    )(own, following)
     received = lax.all_to_all(
         subbands,
         "chan",

time: 25.8 us -> 25.8 us (level)
  waiting for transfers between devices: 4.5 us -> 5.28 us
  Pallas kernels: 4.58 us -> 3.81 us
    ppermute x1, waiting for transfers between devices: 4.5 us -> 5.28 us  [per_device(): lax.ppermute(sent, ('chan', 'tm'), [(c * blocks + z + 1, (c ^ 1) * blocks...]
    pallas_call x2 -> x1, Pallas kernels: 3.24 us -> 2.47 us  [per_device(): pl.pallas_call(beside_kernel, out_shape=[block, jax.ShapeDtypeStruct((Q2...]
  transfers between devices with their start and end apart: 1 -> 1, of which waited for: 1 -> 1; matrix products, arithmetic and copies ran while one was open for 0% -> 0% of each run, Pallas kernels for 13% -> 10%
where the time goes in v9:
time: 25.8 us; the launch traced here: 25.6 us
  blocking collectives  15.2 us (59%)
  waiting for transfers between devices  5.28 us (20%)
  Pallas kernels  3.81 us (15%)
  starting transfers between devices  1.29 us (5%)
    all_to_all x1, blocking collectives, per_device(): lax.all_to_all(subbands, 'chan', split_axis=0, concat_axis=0, tiled=True,...  15.2 us
    ppermute x1, waiting for transfers between devices, per_device(): lax.ppermute(sent, ('chan', 'tm'), [(c * blocks + z + 1, (c ^ 1) * blocks...  5.28 us
    pallas_call x1, Pallas kernels, per_device(): pl.pallas_call(beside_kernel, out_shape=[block, jax.ShapeDtypeStruct((Q2...  2.47 us
    pallas_call x1, Pallas kernels, per_device(): pl.pallas_call(trial_kernel, out_shape=jax.ShapeDtypeStruct((count, trial...  1.3 us
    ppermute x1, starting transfers between devices, per_device(): lax.ppermute(sent, ('chan', 'tm'), [(c * blocks + z + 1, (c ^ 1) * blocks...  1.29 us
  transfers between devices with their start and end apart: 1, of which 1 were waited for; matrix products, arithmetic and copies ran while one was open for 0% of the time, Pallas kernels for 10%

profile of v9, /device:TPU:1, one launch (start us, length us, event | category | flops | bytes accessed | tf_op | source)
XLA Modules:
  0.0 25.6 jit_solution(10470053863163547871)
XLA Ops:
  0.0 1.3 %collective-permute-start = (bf16[64,256]{1,0:T(8,128)(2,1)S(1)}, bf16[64,256]{1,0:T(8,128)(2,1)S(1)}, u32[]{:S(2)}, u32[]{:S(2)}) collective-permute-start(bf16[64,256]{1,0:T(8,128)(2,1)S(1)} %get-tuple-element.13), channel_id=1, source_target_pairs={{1,8},{2,9},{3,10},{4,11},{5,12},{6,13},{7,14},{9,0},{10,1},{11,2}... | collective-permute-start | bytes 98312 | tf_op jit(solution)/shard_map/ppermute | solution.py:227
  1.3 2.5 %beside.1 = (f32[64,256]{1,0:T(8,128)S(1)}, bf16[256,256]{1,0:T(8,128)(2,1)S(1)}, bf16[256,1024]{1,0:T(8,128)(2,1)S(1)}, f32[8,128]{1,0:T(8,128)S(1)}) custom-call(bf16[256,256]{1,0:T(8,128)(2,1)} %spectra_hbm.3, s32[64,256]{1,0:T(8,128)} %bitcast.9, f32[64,256]{1,0:T(8,128)S(1)} %get-tuple-element.11.sums_ref, ...), custom_call_target="tpu_custom_call", output_to_operand_aliasing={{0}: (2, {})} | custom-call | flops 1073741824 | bytes 1048576 | tf_op jit(solution)/shard_map/beside/pallas_call | solution.py:236
  3.8 5.3 %collective-permute-done.next_ref = bf16[64,256]{1,0:T(8,128)(2,1)S(1)} collective-permute-done((bf16[64,256]{1,0:T(8,128)(2,1)S(1)}, bf16[64,256]{1,0:T(8,128)(2,1)S(1)}, u32[]{:S(2)}, u32[]{:S(2)}) %collective-permute-start) | collective-permute-done | bytes 32800 | tf_op jit(solution)/shard_map/ppermute | solution.py:227
  9.1 15.2 %all_to_all.11 = bf16[64,4,128]{2,1,0:T(4,128)(2,1)S(1)} all-to-all(bf16[64,4,128]{2,1,0:T(4,128)(2,1)S(1)} %bitcast.6), channel_id=1, replica_groups={{344,336,360,352,376,368,392,384,408,400,424,416,440,432,456,448,472,46..., dimensions={0} | all-to-all | bytes 131072 | tf_op jit(solution)/shard_map/all_to_all | solution.py:266
  24.3 1.3 %trials.1 = bf16[8,32,256]{2,1,0:T(8,128)(2,1)} custom-call(bf16[256,128]{1,0:T(8,128)(2,1)S(1)} %bitcast.7, bf16[256,256]{1,0:T(8,128)(2,1)S(1)} %get-tuple-element.14.selector_ref, bf16[256,1024]{1,0:T(8,128)(2,1)S(1)} %get-tuple-element.15.band_ref, f32[8,128]{1,0:T(8,128)S(1)} %get-tuple-element.16.scale_ref), custom_call_target="tpu_custom_call" | custom-call | tf_op jit(solution)/shard_map/trials/pallas_call | solution.py:274
  (2 shorter events, 0.0 us)
Async XLA Ops:
  0.0 9.1 %collective-permute-start = (bf16[64,256]{1,0:T(8,128)(2,1)S(1)}, bf16[64,256]{1,0:T(8,128)(2,1)S(1)}, u32[]{:S(2)}, u32[]{:S(2)}) collective-permute-start(bf16[64,256]{1,0:T(8,128)(2,1)S(1)} %get-tuple-element.13), channel_id=1, source_target_pairs={{1,8},{2,9},{3,10},{4,11},{5,12},{6,13},{7,14},{9,0},{10,1},{11,2}... | collective-permute-start | bytes 98312 | tf_op jit(solution)/shard_map/ppermute | solution.py:227

commit v10 on v9

--- a/solution.py
+++ b/solution.py
@@ -53,9 +53,12 @@
     spectra_hbm, delay_hbm, out_ref, sent_ref,
     spectra_ref, delay_ref, acc_ref, before_ref, sems,
 ):
-    copies = [
-        pltpu.make_async_copy(spectra_hbm, spectra_ref, sems.at[0]),
-        pltpu.make_async_copy(delay_hbm, delay_ref, sems.at[1]),
+    half = spectra_ref.shape[0] // 2
+    copies = [pltpu.make_async_copy(delay_hbm, delay_ref, sems.at[0])] + [
+        pltpu.make_async_copy(
+            spectra_hbm.at[pl.ds(half * i, half)], spectra_ref.at[pl.ds(half * i, half)], sems.at[i + 1]
+        )
+        for i in range(2)
     ]
     for copy in copies:
         copy.start()
@@ -210,7 +213,7 @@
         pltpu.VMEM(by_block.shape, by_block.dtype),
         pltpu.VMEM((Q1 * nblk, steps), jnp.float32),
         pltpu.VMEM((Q1 * nblk, LANES), jnp.float32),
-        pltpu.SemaphoreType.DMA((2,)),
+        pltpu.SemaphoreType.DMA((3,)),
     ]
     sources = [pltpu.with_memory_space_constraint(x, pltpu.HBM) for x in (spectra, by_block)]
     own, sent = pl.pallas_call(

time: 25.8 us -> 25.9 us (level)
  no operation moved by 1% of the time
where the time goes in v10:
time: 25.9 us; the launch traced here: 25.6 us
  blocking collectives  15.2 us (59%)
  waiting for transfers between devices  5.27 us (20%)
  Pallas kernels  3.82 us (15%)
  starting transfers between devices  1.29 us (5%)
    all_to_all x1, blocking collectives, per_device(): lax.all_to_all(subbands, 'chan', split_axis=0, concat_axis=0, tiled=True,...  15.2 us
    ppermute x1, waiting for transfers between devices, per_device(): lax.ppermute(sent, ('chan', 'tm'), [(c * blocks + z + 1, (c ^ 1) * blocks...  5.27 us
    pallas_call x1, Pallas kernels, per_device(): pl.pallas_call(beside_kernel, out_shape=[block, jax.ShapeDtypeStruct((Q2...  2.47 us
    pallas_call x1, Pallas kernels, per_device(): pl.pallas_call(trial_kernel, out_shape=jax.ShapeDtypeStruct((count, trial...  1.3 us
    ppermute x1, starting transfers between devices, per_device(): lax.ppermute(sent, ('chan', 'tm'), [(c * blocks + z + 1, (c ^ 1) * blocks...  1.29 us
  transfers between devices with their start and end apart: 1, of which 1 were waited for; matrix products, arithmetic and copies ran while one was open for 0% of the time, Pallas kernels for 10%

profile of v10, /device:TPU:1, one launch (start us, length us, event | category | flops | bytes accessed | tf_op | source)
XLA Modules:
  0.0 25.6 jit_solution(16919375648646143902)
XLA Ops:
  0.0 1.3 %collective-permute-start = (bf16[64,256]{1,0:T(8,128)(2,1)S(1)}, bf16[64,256]{1,0:T(8,128)(2,1)S(1)}, u32[]{:S(2)}, u32[]{:S(2)}) collective-permute-start(bf16[64,256]{1,0:T(8,128)(2,1)S(1)} %get-tuple-element.13), channel_id=1, source_target_pairs={{1,8},{2,9},{3,10},{4,11},{5,12},{6,13},{7,14},{9,0},{10,1},{11,2}... | collective-permute-start | bytes 98312 | tf_op jit(solution)/shard_map/ppermute | solution.py:230
  1.3 2.5 %beside.1 = (f32[64,256]{1,0:T(8,128)S(1)}, bf16[256,256]{1,0:T(8,128)(2,1)S(1)}, bf16[256,1024]{1,0:T(8,128)(2,1)S(1)}, f32[8,128]{1,0:T(8,128)S(1)}) custom-call(bf16[256,256]{1,0:T(8,128)(2,1)} %spectra_hbm.3, s32[64,256]{1,0:T(8,128)} %bitcast.9, f32[64,256]{1,0:T(8,128)S(1)} %get-tuple-element.11.sums_ref, ...), custom_call_target="tpu_custom_call", output_to_operand_aliasing={{0}: (2, {})} | custom-call | flops 1073741824 | bytes 1048576 | tf_op jit(solution)/shard_map/beside/pallas_call | solution.py:239
  3.8 5.3 %collective-permute-done.next_ref = bf16[64,256]{1,0:T(8,128)(2,1)S(1)} collective-permute-done((bf16[64,256]{1,0:T(8,128)(2,1)S(1)}, bf16[64,256]{1,0:T(8,128)(2,1)S(1)}, u32[]{:S(2)}, u32[]{:S(2)}) %collective-permute-start) | collective-permute-done | bytes 32800 | tf_op jit(solution)/shard_map/ppermute | solution.py:230
  9.1 15.2 %all_to_all.11 = bf16[64,4,128]{2,1,0:T(4,128)(2,1)S(1)} all-to-all(bf16[64,4,128]{2,1,0:T(4,128)(2,1)S(1)} %bitcast.6), channel_id=1, replica_groups={{344,336,360,352,376,368,392,384,408,400,424,416,440,432,456,448,472,46..., dimensions={0} | all-to-all | bytes 131072 | tf_op jit(solution)/shard_map/all_to_all | solution.py:269
  24.3 1.3 %trials.1 = bf16[8,32,256]{2,1,0:T(8,128)(2,1)} custom-call(bf16[256,128]{1,0:T(8,128)(2,1)S(1)} %bitcast.7, bf16[256,256]{1,0:T(8,128)(2,1)S(1)} %get-tuple-element.14.selector_ref, bf16[256,1024]{1,0:T(8,128)(2,1)S(1)} %get-tuple-element.15.band_ref, f32[8,128]{1,0:T(8,128)S(1)} %get-tuple-element.16.scale_ref), custom_call_target="tpu_custom_call" | custom-call | tf_op jit(solution)/shard_map/trials/pallas_call | solution.py:277
  (2 shorter events, 0.0 us)
Async XLA Ops:
  0.0 9.1 %collective-permute-start = (bf16[64,256]{1,0:T(8,128)(2,1)S(1)}, bf16[64,256]{1,0:T(8,128)(2,1)S(1)}, u32[]{:S(2)}, u32[]{:S(2)}) collective-permute-start(bf16[64,256]{1,0:T(8,128)(2,1)S(1)} %get-tuple-element.13), channel_id=1, source_target_pairs={{1,8},{2,9},{3,10},{4,11},{5,12},{6,13},{7,14},{9,0},{10,1},{11,2}... | collective-permute-start | bytes 98312 | tf_op jit(solution)/shard_map/ppermute | solution.py:230
